TPU v7x, 32 devices: a whole 2x2x4 slice. The times are simulated.
32 devices in a mesh: grid: 32 (over z, y, x, core), day: 1.
Axes of the slice: x: 2, y: 2, z: 4, core: 2. Of those that a mesh axis runs over, the one named last changes fastest.
Arguments:
- fields: bfloat16 [384, 131072], P('day', 'grid')
- eof_basis: bfloat16 [131072, 128], P('grid'), may hold values from -0.015625 to 0.015625
- seed_days: int32 [16], replicated, may hold values from 0 to 383, as said below
Outputs:
- memberships: float32 [384, 16], P('day')
- regime_centers: float32 [16, 128], replicated
- composites: float32 [16, 131072], P(None, 'grid')
Inputs may be any that keep to these rules, and one draw needn't show every extreme that they name: `seed_days`: 16 distinct days of the record.
All inputs are finite; a program needn't handle non-finite values.
Results may differ from a plain program's by a relative error of at most 0.00043.
Values sent between devices are 32-bit elements; how exact they have to be, the bound alone decides.
A program may use at most 64 MiB of HBM per device.

v0:
```python
import jax
import jax.numpy as jnp
from jax import lax
from jax.sharding import PartitionSpec as P

ITERS = 3


def member_of(amplitudes, centers):
    offsets = amplitudes[:, None, :] - centers[None, :, :]
    mean_square = jnp.mean(offsets * offsets, axis=2) + 1e-05
    weights = 1.0 / mean_square
    return weights / jnp.sum(weights, axis=1, keepdims=True)


def seed_terms(seed_days, first, amplitudes):
    positions = first + jnp.arange(amplitudes.shape[0], dtype=jnp.int32)
    selector = (seed_days[:, None] == positions[None, :]).astype(jnp.float32)
    return jnp.dot(selector, amplitudes, precision=lax.Precision.HIGHEST)


def regime_terms(amplitudes, centers):
    member = member_of(amplitudes, centers)
    squared = member * member
    numerator = jnp.dot(squared.T, amplitudes, precision=lax.Precision.HIGHEST)
    return (numerator, jnp.sum(squared, axis=0))


def on_device(fields, eof_basis, seed_days):
    day_rows = fields.shape[0]
    partial_value = jnp.dot(fields, eof_basis, preferred_element_type=jnp.float32)
    amplitudes = lax.psum(partial_value, "grid")
    first = lax.axis_index("day") * day_rows
    centers = lax.psum(seed_terms(seed_days, first, amplitudes), "day")
    for sweep in range(ITERS):
        numerator, denominator = lax.psum(regime_terms(amplitudes, centers), "day")
        centers = numerator / denominator[:, None]
    member_all = member_of(amplitudes, centers)
    squares = member_all * member_all
    weights_bf = squares.astype(jnp.bfloat16)
    weighted = jnp.dot(weights_bf.T, fields, preferred_element_type=jnp.float32)
    totals, weight_sums = lax.psum((weighted, jnp.sum(squares, axis=0)), "day")
    return (member_all, centers, totals / weight_sums[:, None])


def solution(mesh):
    placed = (P("day", "grid"), P("grid", None), P())
    return jax.shard_map(
        on_device,
        mesh=mesh,
        in_specs=placed,
        out_specs=(P("day", None), P(), P(None, "grid")),
        check_vma=False,
    )
```

profile of v0, /device:TPU:0, one launch (start us, length us, event | category | flops | bytes accessed | tf_op | source)
XLA Modules:
  0.0 160.0 jit_solution(17271078939652637801)
XLA Ops:
  7.2 0.0 copy-start
  7.2 0.0 copy-start.3
  7.2 0.0 all-reduce.2.cloned.1.call-start
  7.2 1.8 %copy-done = bf16[384,4096]{1,0:T(8,128)(2,1)S(1)} copy-done((bf16[384,4096]{1,0:T(8,128)(2,1)S(1)}, bf16[384,4096]{1,0:T(8,128)(2,1)}, u32[]{:S(2)}) %copy-start) | copy-done | bytes 3145752
  9.1 2.9 %fusion.5 = f32[384,128]{1,0:T(8,128)} fusion(bf16[384,4096]{1,0:T(8,128)(2,1)S(1)} %copy-done, bf16[4096,128]{1,0:T(8,128)(2,1)} %param.4), kind=kOutput, calls=%fused_computation.28 | convolution fusion | flops 402653184 | bytes 4390912 | tf_op jit(solution)/shard_map/dot_general | solution.py:31
  11.9 0.0 all-reduce.2.cloned.1.call-update
  12.0 127.8 %all-reduce.2.cloned.1.call-done = f32[384,128]{1,0:T(8,128)} async-done(((f32[384,128]{1,0:T(8,128)}), f32[384,128]{1,0:T(8,128)}) %all-reduce.2.cloned.1.call-update) | async-done | bytes 196624 | tf_op jit(solution)/shard_map/psum | solution.py:32
  139.8 0.0 copy-done.3
  139.8 0.0 copy-start.1
  139.8 1.2 fusion
  141.0 1.8 %multiply_reduce_fusion.3 = f32[384,16]{1,0:T(8,128)S(1)} fusion(f32[16,128]{1,0:T(8,128)S(1)} %fusion, f32[384,128]{1,0:T(8,128)} %all-reduce.2.cloned.1.call-done), kind=kLoop, calls=%fused_computation.4 | loop fusion | flops 2353152 | bytes 229376 | tf_op jit(solution)/shard_map/reduce_sum | solution.py:11
  142.9 0.2 divide_reduce_fusion.3
  143.0 0.1 fusion.2
  143.2 1.4 convolution_divide_fusion.3
  144.6 1.9 %multiply_reduce_fusion.2 = f32[384,16]{1,0:T(8,128)S(1)} fusion(f32[16,128]{1,0:T(8,128)S(1)} %convolution_divide_fusion.3, f32[384,128]{1,0:T(8,128)} %all-reduce.2.cloned.1.call-done), kind=kLoop, calls=%fused_computation.3 | loop fusion | flops 2353152 | bytes 229376 | tf_op jit(solution)/shard_map/reduce_sum | solution.py:11
  146.5 0.2 divide_reduce_fusion.2
  146.6 0.1 fusion.3
  146.8 1.4 convolution_divide_fusion.2
  148.2 0.0 copy-done.1
  148.2 0.9 multiply_reduce_fusion.1
  149.1 0.2 divide_reduce_fusion.1
  149.3 0.1 fusion.4
  149.4 0.5 convolution_divide_fusion.1
  150.0 0.0 copy-start.2
  150.0 0.9 multiply_reduce_fusion
  150.9 0.2 divide_reduce_fusion
  151.0 0.1 multiply_reduce_fusion.4
  151.2 0.7 copy.6
  151.9 1.2 convolution_divide_fusion
  153.2 0.0 copy-done.2
Async XLA Ops:
  7.2 1.9 %copy-start = (bf16[384,4096]{1,0:T(8,128)(2,1)S(1)}, bf16[384,4096]{1,0:T(8,128)(2,1)}, u32[]{:S(2)}) copy-start(bf16[384,4096]{1,0:T(8,128)(2,1)} %param.3) | copy-start | bytes 9437188
  7.2 132.6 %copy-start.3 = (s32[16]{0:T(128)S(1)}, s32[16]{0:T(128)}, u32[]{:S(2)}) copy-start(s32[16]{0:T(128)} %param.5) | copy-start | bytes 196
  7.2 132.6 %all-reduce.2.cloned.1.call-start = ((), (), s32[]{:S(2)}) async-start(), calls=%async_computation | async-start | bytes 393216 | tf_op jit(solution)/shard_map/psum | solution.py:32
  139.8 8.4 %copy-start.1 = (f32[384,128]{1,0:T(8,128)S(1)}, f32[384,128]{1,0:T(8,128)}, u32[]{:S(2)}) copy-start(f32[384,128]{1,0:T(8,128)} %all-reduce.2.cloned.1.call-done) | copy-start | bytes 589828
  150.0 3.2 %copy-start.2 = (f32[16,128]{1,0:T(8,128)}, f32[16,128]{1,0:T(8,128)S(1)}, u32[]{:S(2)}) copy-start(f32[16,128]{1,0:T(8,128)S(1)} %convolution_divide_fusion.1) | copy-start | bytes 24580
Sparse Core Ops, SparseCore 0:
  14.1 125.6 all-reduce.1
where the time goes:
time: 161 us; the launch traced here: 160 us
  waiting for transfers between devices  128 us (80%)
  between operations  14.1 us (9%)
  matrix products  8.77 us (5%)
  other arithmetic  6.67 us (4%)
  local copies, waits for them, and re-layouts  2.57 us (2%)
    psum x1, waiting for transfers between devices, on_device(): amplitudes = lax.psum(partial_value, 'grid')  128 us
    reduce_sum x4, other arithmetic, member_of(): mean_square = jnp.mean(offsets * offsets, axis=2) + 1e-05  5.48 us
    dot_general x3, matrix products, regime_terms(): numerator = jnp.dot(squared.T, amplitudes, precision=lax.Precision.HIGHEST)  3.42 us
  transfers between devices with their start and end apart: 1, of which 1 were waited for; matrix products, arithmetic and copies ran while one was open for 0% of the time, Pallas kernels for 0%

commit v1 on v0

--- a/solution.py
+++ b/solution.py
@@ -1,9 +1,16 @@
+import functools
+
 import jax
 import jax.numpy as jnp
 from jax import lax
+from jax.experimental import pallas as pl
+from jax.experimental.pallas import tpu as pltpu
 from jax.sharding import PartitionSpec as P
 
 ITERS = 3
+CHUNKS = 2
+VMEM_BYTES = 48 * 1024 * 1024
+NT = (((1,), (1,)), ((), ()))
 
 
 def member_of(amplitudes, centers):
@@ -26,10 +33,228 @@
     return (numerator, jnp.sum(squared, axis=0))
 
 
-def on_device(fields, eof_basis, seed_days):
+def amplitude_kernel(n, fields, basis, out, fbuf, bbuf, give, take, mine, parts, gathered,
+                     load_sems, pair_sems, scatter_send, scatter_recv, gather_send, gather_recv):
+    pairs = n // 2
+    rows = out.shape[0]
+    half = rows // 2
+    piece = half // CHUNKS
+    block = rows // n
+    me = lax.axis_index("grid")
+    core = lax.rem(me, 2)
+    spot = me // 2
+    partner = me + 1 - 2 * core
+
+    def at(other_spot):
+        return {"grid": 2 * other_spot + core}
+
+    barrier = pltpu.get_barrier_semaphore()
+    pl.semaphore_signal(barrier, inc=1, device_id={"grid": partner}, device_id_type=pl.DeviceIdType.MESH)
+    for step in range(1, pairs):
+        pl.semaphore_signal(barrier, inc=1, device_id=at(lax.rem(spot + step, pairs)),
+                            device_id_type=pl.DeviceIdType.MESH)
+
+    basis_load = pltpu.make_async_copy(basis, bbuf, load_sems.at[2 * CHUNKS])
+    basis_load.start()
+    loads = []
+    for i in range(2 * CHUNKS):
+        side = 1 - core if i < CHUNKS else core
+        first = pl.multiple_of(side * half + (i % CHUNKS) * piece, 16)
+        load = pltpu.make_async_copy(fields.at[pl.ds(first, piece)], fbuf.at[pl.ds(i * piece, piece)],
+                                     load_sems.at[i])
+        load.start()
+        loads.append(load)
+    basis_load.wait()
+
+    def product(i):
+        loads[i].wait()
+        return jnp.dot(fbuf[i * piece:(i + 1) * piece, :], bbuf[...], preferred_element_type=jnp.float32)
+
+    for i in range(CHUNKS):
+        give[i * piece:(i + 1) * piece, :] = product(i)
+    pl.semaphore_wait(barrier, pairs)
+    pair_give = pltpu.make_async_remote_copy(
+        src_ref=give, dst_ref=take, send_sem=pair_sems.at[0], recv_sem=pair_sems.at[1],
+        device_id={"grid": partner}, device_id_type=pl.DeviceIdType.MESH)
+    pair_give.start()
+    own = [product(CHUNKS + i) for i in range(CHUNKS)]
+    pair_give.wait_recv()
+    total = jnp.concatenate(own, axis=0) + take[...]
+    for j in range(pairs):
+        mine[j] = total[j * block:(j + 1) * block, :]
+
+    scatters = []
+    for step in range(1, pairs):
+        to = lax.rem(spot + step, pairs)
+        copy = pltpu.make_async_remote_copy(
+            src_ref=mine.at[to], dst_ref=parts.at[spot], send_sem=scatter_send.at[step],
+            recv_sem=scatter_recv.at[spot], device_id=at(to), device_id_type=pl.DeviceIdType.MESH)
+        copy.start()
+        scatters.append(copy)
+    parts[spot] = mine[spot]
+    for step in range(1, pairs):
+        source = lax.rem(spot + pairs - step, pairs)
+        pltpu.make_async_remote_copy(
+            src_ref=mine.at[source], dst_ref=parts.at[source], send_sem=scatter_send.at[step],
+            recv_sem=scatter_recv.at[source], device_id=at(source),
+            device_id_type=pl.DeviceIdType.MESH).wait_recv()
+    gathered[core, spot] = jnp.sum(parts[...], axis=0)
+
+    gathers = []
+    for step in range(1, pairs):
+        to = lax.rem(spot + step, pairs)
+        copy = pltpu.make_async_remote_copy(
+            src_ref=gathered.at[core, spot], dst_ref=gathered.at[core, spot], send_sem=gather_send.at[step],
+            recv_sem=gather_recv.at[spot], device_id=at(to), device_id_type=pl.DeviceIdType.MESH)
+        copy.start()
+        gathers.append(copy)
+    for step in range(1, pairs):
+        source = lax.rem(spot + pairs - step, pairs)
+        pltpu.make_async_remote_copy(
+            src_ref=gathered.at[core, source], dst_ref=gathered.at[core, source],
+            send_sem=gather_send.at[step], recv_sem=gather_recv.at[source], device_id=at(source),
+            device_id_type=pl.DeviceIdType.MESH).wait_recv()
+    pair_back = pltpu.make_async_remote_copy(
+        src_ref=gathered.at[core], dst_ref=gathered.at[core], send_sem=pair_sems.at[2],
+        recv_sem=pair_sems.at[3], device_id={"grid": partner}, device_id_type=pl.DeviceIdType.MESH)
+    pair_back.start()
+    pltpu.make_async_remote_copy(
+        src_ref=gathered.at[1 - core], dst_ref=gathered.at[1 - core], send_sem=pair_sems.at[2],
+        recv_sem=pair_sems.at[3], device_id={"grid": partner},
+        device_id_type=pl.DeviceIdType.MESH).wait_recv()
+    for side in range(2):
+        for j in range(pairs):
+            first = side * half + j * block
+            out[first:first + block, :] = gathered[side, j]
+    pair_give.wait_send()
+    pair_back.wait_send()
+    for copy in scatters + gathers:
+        copy.wait_send()
+
+
+def summed_amplitudes(n, fields, basis):
+    rows, depth = fields.shape
+    eofs = basis.shape[1]
+    pairs, half, block = n // 2, rows // 2, rows // n
+    return pl.pallas_call(
+        functools.partial(amplitude_kernel, n),
+        out_shape=jax.ShapeDtypeStruct((rows, eofs), jnp.float32),
+        in_specs=[pl.BlockSpec(memory_space=pl.ANY)] * 2,
+        out_specs=pl.BlockSpec(memory_space=pltpu.VMEM),
+        scratch_shapes=[
+            pltpu.VMEM((rows, depth), jnp.bfloat16),
+            pltpu.VMEM((depth, eofs), jnp.bfloat16),
+            pltpu.VMEM((half, eofs), jnp.float32),
+            pltpu.VMEM((half, eofs), jnp.float32),
+            pltpu.VMEM((pairs, block, eofs), jnp.float32),
+            pltpu.VMEM((pairs, block, eofs), jnp.float32),
+            pltpu.VMEM((2, pairs, block, eofs), jnp.float32),
+            pltpu.SemaphoreType.DMA((2 * CHUNKS + 1,)),
+            pltpu.SemaphoreType.DMA((4,)),
+            pltpu.SemaphoreType.DMA((pairs,)),
+            pltpu.SemaphoreType.DMA((pairs,)),
+            pltpu.SemaphoreType.DMA((pairs,)),
+            pltpu.SemaphoreType.DMA((pairs,)),
+        ],
+        compiler_params=pltpu.CompilerParams(
+            collective_id=0, has_side_effects=True, vmem_limit_bytes=VMEM_BYTES),
+        cost_estimate=pl.CostEstimate(
+            flops=2 * rows * depth * eofs, bytes_accessed=2 * depth * (rows + eofs), transcendentals=0),
+    )(fields, basis)
+
+
+def split(value, pieces):
+    out = []
+    for _ in range(pieces):
+        part = value.astype(jnp.bfloat16)
+        out.append(part)
+        value = value - part.astype(jnp.float32)
+    return out
+
+
+def regime_kernel(seeds, amplitudes, fields, member_out, centers_out, composites, fbuf, load_sems):
+    days, eofs = amplitudes.shape
+    regimes = centers_out.shape[0]
+    piece = days // CHUNKS
+    loads = []
+    for i in range(CHUNKS):
+        load = pltpu.make_async_copy(fields.at[pl.ds(i * piece, piece)], fbuf.at[pl.ds(i * piece, piece)],
+                                     load_sems.at[i])
+        load.start()
+        loads.append(load)
+
+    turned = amplitudes[...].T
+    with_ones = jnp.concatenate([turned, jnp.ones((8, days), jnp.float32)], axis=0)
+    first, second, third = split(with_ones, 3)
+    exact = jnp.concatenate([first, second, third], axis=1)
+    five = jnp.concatenate([exact, first, second], axis=1)
+
+    def member(columns):
+        squares = []
+        for c in range(regimes):
+            offset = turned - columns[:, c:c + 1]
+            squares.append(jnp.sum(offset * offset, axis=0, keepdims=True))
+        mean_square = jnp.concatenate(squares, axis=0) * (1.0 / eofs) + 1e-05
+        weights = 1.0 / mean_square
+        return weights / jnp.sum(weights, axis=0, keepdims=True)
+
+    positions = lax.broadcasted_iota(jnp.int32, (regimes, days), 1)
+    selector = (seeds[...] == positions).astype(jnp.bfloat16)
+    columns = lax.dot_general(exact, jnp.concatenate([selector] * 3, axis=1), NT,
+                              preferred_element_type=jnp.float32)[:eofs]
+    for sweep in range(ITERS):
+        q = member(columns)
+        high, low = split(q * q, 2)
+        weights = jnp.concatenate([high, high, high, low, low], axis=1)
+        sums = lax.dot_general(five, weights, NT, preferred_element_type=jnp.float32)
+        columns = sums[:eofs] / sums[eofs:eofs + 1]
+        if sweep == ITERS - 1:
+            flat = lax.dot_general(weights, five, NT, preferred_element_type=jnp.float32)
+            centers_out[...] = flat[:, :eofs] / flat[:, eofs:eofs + 1]
+    final = member(columns)
+    squares = final * final
+    scale = 1.0 / jnp.sum(squares, axis=1, keepdims=True)
+    weights_bf = squares.astype(jnp.bfloat16)
+    member_out[...] = final.T
+    for load in loads:
+        load.wait()
+    composites[...] = jnp.dot(weights_bf, fbuf[...], preferred_element_type=jnp.float32) * scale
+
+
+def regimes_of(seed_days, amplitudes, fields):
+    days, points = fields.shape
+    eofs = amplitudes.shape[1]
+    regimes = seed_days.shape[0]
+    vmem = pl.BlockSpec(memory_space=pltpu.VMEM)
+    return pl.pallas_call(
+        regime_kernel,
+        out_shape=(
+            jax.ShapeDtypeStruct((days, regimes), jnp.float32),
+            jax.ShapeDtypeStruct((regimes, eofs), jnp.float32),
+            jax.ShapeDtypeStruct((regimes, points), jnp.float32),
+        ),
+        in_specs=[vmem, vmem, pl.BlockSpec(memory_space=pl.ANY)],
+        out_specs=(vmem, vmem, vmem),
+        scratch_shapes=[
+            pltpu.VMEM((days, points), jnp.bfloat16),
+            pltpu.SemaphoreType.DMA((CHUNKS,)),
+        ],
+        compiler_params=pltpu.CompilerParams(vmem_limit_bytes=VMEM_BYTES),
+        cost_estimate=pl.CostEstimate(
+            flops=2 * regimes * days * points, bytes_accessed=2 * days * points, transcendentals=0),
+    )(seed_days.reshape(regimes, 1), amplitudes, fields)
+
+
+def on_device(mesh, fields, eof_basis, seed_days):
+    n = mesh.shape["grid"]
     day_rows = fields.shape[0]
-    partial_value = jnp.dot(fields, eof_basis, preferred_element_type=jnp.float32)
-    amplitudes = lax.psum(partial_value, "grid")
+    if n % 2 == 0 and n >= 4 and day_rows % (32 * CHUNKS) == 0 and day_rows % n == 0:
+        amplitudes = summed_amplitudes(n, fields, eof_basis)
+    else:
+        partial_value = jnp.dot(fields, eof_basis, preferred_element_type=jnp.float32)
+        amplitudes = lax.psum(partial_value, "grid")
+    if mesh.shape["day"] == 1 and day_rows % 128 == 0 and eof_basis.shape[1] % 128 == 0:
+        return regimes_of(seed_days, amplitudes, fields)
     first = lax.axis_index("day") * day_rows
     centers = lax.psum(seed_terms(seed_days, first, amplitudes), "day")
     for sweep in range(ITERS):
@@ -46,7 +271,7 @@
 def solution(mesh):
     placed = (P("day", "grid"), P("grid", None), P())
     return jax.shard_map(
-        on_device,
+        functools.partial(on_device, mesh),
         mesh=mesh,
         in_specs=placed,
         out_specs=(P("day", None), P(), P(None, "grid")),

time: 161 us -> 30.3 us (0.19)
  waiting for transfers between devices: 128 us -> 0 us
  Pallas kernels: 0 us -> 24.9 us
  between operations: 14.1 us -> 0.65 us
  matrix products: 8.77 us -> 0 us
  other arithmetic: 6.67 us -> 0 us
  local copies, waits for them, and re-layouts: 2.57 us -> 4.56 us
    psum x1 -> x0, waiting for transfers between devices: 128 us -> none  [on_device(): amplitudes = lax.psum(partial_value, 'grid')]
    pallas_call x0 -> x2, Pallas kernels: none -> 24.9 us  [the longest x1 19.6 us: summed_amplitudes(): pl.pallas_call(functools.partial(amplitude_kernel, n), out_shape=jax.Shap...]
    dot_general x6 -> x0, matrix products: 8.77 us -> none  [the longest x3 3.42 us: regime_terms(): numerator = jnp.dot(squared.T, amplitudes, precision=lax.Precision.HIGHEST)]
    reduce_sum x12 -> x0, other arithmetic: 6.67 us -> none  [the longest x4 5.48 us: member_of(): mean_square = jnp.mean(offsets * offsets, axis=2) + 1e-05]
  transfers between devices with their start and end apart: 1 -> 0, of which waited for: 1 -> 0; matrix products, arithmetic and copies ran while one was open for 0% -> 0% of each run, Pallas kernels for 0% -> 0%
where the time goes in v1:
time: 30.3 us; the launch traced here: 30.1 us
  Pallas kernels  24.9 us (82%)
  local copies, waits for them, and re-layouts  4.56 us (15%)
  between operations  0.65 us (2%)
    pallas_call x1, Pallas kernels, summed_amplitudes(): pl.pallas_call(functools.partial(amplitude_kernel, n), out_shape=jax.Shap...  19.6 us
    pallas_call x1, Pallas kernels, regimes_of(): pl.pallas_call(regime_kernel, out_shape=(jax.ShapeDtypeStruct((days, regi...  5.28 us
    unnamed x4, local copies, waits for them, and re-layouts  3.11 us
    reshape x1, local copies, waits for them, and re-layouts, regimes_of(): seed_days.reshape(regimes, 1)  0.73 us
    pallas_call x1, local copies, waits for them, and re-layouts, regimes_of(): pl.pallas_call(regime_kernel, out_shape=(jax.ShapeDtypeStruct((days, regi...  0.71 us

profile of v1, /device:TPU:0, one launch (start us, length us, event | category | flops | bytes accessed | tf_op | source)
XLA Modules:
  0.0 30.1 jit_solution(12736912063941851238)
XLA Ops:
  0.6 0.7 %copy.6.seeds = s32[16,1]{1,0:T(8,128)S(1)} copy(s32[16,1]{0,1:T(1,128)} %bitcast.1) | data formatting | bytes 128 | tf_op jit(solution)/shard_map/reshape | solution.py:245
  1.4 0.0 copy-start
  1.4 1.9 %copy-done = bf16[384,4096]{1,0:T(8,128)(2,1)S(1)} copy-done((bf16[384,4096]{1,0:T(8,128)(2,1)S(1)}, bf16[384,4096]{1,0:T(8,128)(2,1)}, u32[]{:S(2)}) %copy-start) | copy-done | bytes 3145752
  3.3 0.0 copy-start.1
  3.3 1.2 %copy-done.1 = bf16[4096,128]{1,0:T(8,128)(2,1)S(1)} copy-done((bf16[4096,128]{1,0:T(8,128)(2,1)S(1)}, bf16[4096,128]{1,0:T(8,128)(2,1)}, u32[]{:S(2)}) %copy-start.1) | copy-done | bytes 1048600
  4.5 19.6 %shard_map.58.amplitudes = f32[384,128]{1,0:T(8,128)S(1)} custom-call(bf16[384,4096]{1,0:T(8,128)(2,1)S(1)} %copy-done, bf16[4096,128]{1,0:T(8,128)(2,1)S(1)} %copy-done.1), custom_call_target="tpu_custom_call" | custom-call | flops 402653184 | bytes 4194304 | tf_op jit(solution)/shard_map/pallas_call | solution.py:139
  24.1 5.3 %shard_map.59 = (f32[384,16]{1,0:T(8,128)S(1)}, f32[16,128]{1,0:T(8,128)}, f32[16,4096]{1,0:T(8,128)}) custom-call(s32[16,1]{1,0:T(8,128)S(1)} %copy.6.seeds, f32[384,128]{1,0:T(8,128)S(1)} %shard_map.58.amplitudes, bf16[384,4096]{1,0:T(8,128)(2,1)S(1)} %copy-done), custom_call_target="tpu_custom_call" | custom-call | flops 50331648 | bytes 3145728 | tf_op jit(solution)/shard_map/pallas_call | solution.py:229
  29.4 0.7 %copy.7 = f32[384,16]{0,1:T(8,128)} copy(f32[384,16]{1,0:T(8,128)S(1)} %get-tuple-element.3) | data formatting | bytes 49152 | tf_op jit(solution)/shard_map/pallas_call | solution.py:229
Async XLA Ops:
  1.4 1.9 %copy-start = (bf16[384,4096]{1,0:T(8,128)(2,1)S(1)}, bf16[384,4096]{1,0:T(8,128)(2,1)}, u32[]{:S(2)}) copy-start(bf16[384,4096]{1,0:T(8,128)(2,1)} %fields.3) | copy-start | bytes 9437188
  3.3 1.2 %copy-start.1 = (bf16[4096,128]{1,0:T(8,128)(2,1)S(1)}, bf16[4096,128]{1,0:T(8,128)(2,1)}, u32[]{:S(2)}) copy-start(bf16[4096,128]{1,0:T(8,128)(2,1)} %basis.1) | copy-start | bytes 3145732

commit v2 on v1

v2 whole, which is shorter than its diff:
```python
import functools

import jax
import jax.numpy as jnp
from jax import lax
from jax.experimental import pallas as pl
from jax.experimental.pallas import tpu as pltpu
from jax.sharding import PartitionSpec as P

ITERS = 3
CHUNKS = 2
VMEM_BYTES = 63 * 1024 * 1024 + 512 * 1024
NT = (((1,), (1,)), ((), ()))


def member_of(amplitudes, centers):
    offsets = amplitudes[:, None, :] - centers[None, :, :]
    mean_square = jnp.mean(offsets * offsets, axis=2) + 1e-05
    weights = 1.0 / mean_square
    return weights / jnp.sum(weights, axis=1, keepdims=True)


def seed_terms(seed_days, first, amplitudes):
    positions = first + jnp.arange(amplitudes.shape[0], dtype=jnp.int32)
    selector = (seed_days[:, None] == positions[None, :]).astype(jnp.float32)
    return jnp.dot(selector, amplitudes, precision=lax.Precision.HIGHEST)


def regime_terms(amplitudes, centers):
    member = member_of(amplitudes, centers)
    squared = member * member
    numerator = jnp.dot(squared.T, amplitudes, precision=lax.Precision.HIGHEST)
    return (numerator, jnp.sum(squared, axis=0))


def amplitude_kernel(lines, fields, basis, out, fbuf, bbuf, give, take, mine, parts, stack, load_sems,
                     pair_send, pair_recv, plane_send, plane_recv, line_send, line_recv,
                     back_send, back_recv, final_send, final_recv):
    rows = out.shape[0]
    half = rows // 2
    block = half // 4
    piece = 2 * block
    me = lax.axis_index("grid")
    core = lax.rem(me, 2)
    spot = me // 2
    plane = lax.rem(spot, 4)
    line = spot // 4
    px, py = lax.rem(plane, 2), plane // 2
    order = [(1 - py) * 2 + 1 - px, (1 - py) * 2 + px, py * 2 + 1 - px, plane]

    def send(src, dst, send_sem, recv_sem, device):
        return pltpu.make_async_remote_copy(
            src_ref=src, dst_ref=dst, send_sem=send_sem, recv_sem=recv_sem,
            device_id={"grid": device}, device_id_type=pl.DeviceIdType.MESH)

    partner = me + 1 - 2 * core
    plane_peers = [(line * 4 + position) * 2 + core for position in order[:3]]
    line_steps = sorted(range(1, lines), key=lambda step: -min(step, lines - step))
    line_peers = [lax.rem(line + step, lines) for step in line_steps]
    line_devices = [(peer * 4 + plane) * 2 + core for peer in line_peers]

    barrier = pltpu.get_barrier_semaphore()
    for device in [partner] + plane_peers + line_devices:
        pl.semaphore_signal(barrier, inc=1, device_id={"grid": device}, device_id_type=pl.DeviceIdType.MESH)

    basis_load = pltpu.make_async_copy(basis, bbuf, load_sems.at[8])
    basis_load.start()
    loads = []
    for i in range(8):
        side = 1 - core if i < 4 else core
        first = pl.multiple_of(side * half + order[i % 4] * block, 16)
        load = pltpu.make_async_copy(fields.at[pl.ds(first, block)], fbuf.at[pl.ds(i * block, block)],
                                     load_sems.at[i])
        load.start()
        loads.append(load)
    basis_load.wait()

    def product(i):
        loads[2 * i].wait()
        loads[2 * i + 1].wait()
        return jnp.dot(fbuf[i * piece:(i + 1) * piece, :], bbuf[...], preferred_element_type=jnp.float32)

    started = []
    pair_copies = []
    for i in range(2):
        part = pl.ds(i * piece, piece)
        give[part, :] = product(i)
        if i == 0:
            pl.semaphore_wait(barrier, 1 + 3 + lines - 1)
        copy = send(give.at[part], take.at[part], pair_send.at[i], pair_recv.at[i], partner)
        copy.start()
        pair_copies.append(copy)
    plane_copies = []
    for i in range(2):
        part = pl.ds(i * piece, piece)
        own = product(2 + i)
        pair_copies[i].wait_recv()
        mine[part, :] = own + take[part, :]
        for k in (2 * i, 2 * i + 1):
            if k < 3:
                copy = send(mine.at[pl.ds(k * block, block)], parts.at[k], plane_send.at[k], plane_recv.at[k],
                            plane_peers[k])
                copy.start()
                plane_copies.append(copy)
    total = mine[3 * block:, :]
    for k in (2, 1, 0):
        plane_copies[k].wait_recv()
        total = total + parts[k]
    stack[line] = total

    for step, device in enumerate(line_devices):
        copy = send(stack.at[line], stack.at[line], line_send.at[step], line_recv.at[line], device)
        copy.start()
        started.append(copy)
    for step in range(lines - 1):
        source = lax.rem(line + lines - line_steps[step], lines)
        send(stack.at[source], stack.at[source], line_send.at[step], line_recv.at[source],
             (source * 4 + plane) * 2 + core).wait_recv()
    total = stack[0]
    for j in range(1, lines):
        total = total + stack[j]

    def place(side, position):
        return out.at[pl.ds(pl.multiple_of(side * half + position * block, 8), block)]

    place(core, plane)[...] = total
    back_copies = []
    for k in range(3):
        copy = send(place(core, plane), place(core, plane), back_send.at[k], back_recv.at[k], plane_peers[k])
        copy.start()
        back_copies.append(copy)
    for k in (3, 2, 1, 0):
        if k < 3:
            send(place(core, order[k]), place(core, order[k]), back_send.at[k], back_recv.at[k],
                 plane_peers[k]).wait_recv()
        copy = send(place(core, order[k]), place(core, order[k]), final_send.at[k], final_recv.at[k], partner)
        copy.start()
        started.append(copy)
    for k in (3, 2, 1, 0):
        send(place(1 - core, order[k]), place(1 - core, order[k]), final_send.at[k], final_recv.at[k],
             partner).wait_recv()
    for copy in pair_copies + plane_copies + started + back_copies:
        copy.wait_send()


def summed_amplitudes(lines, fields, basis):
    rows, depth = fields.shape
    eofs = basis.shape[1]
    half, block = rows // 2, rows // 8
    dma = pltpu.SemaphoreType.DMA
    return pl.pallas_call(
        functools.partial(amplitude_kernel, lines),
        out_shape=jax.ShapeDtypeStruct((rows, eofs), jnp.float32),
        in_specs=[pl.BlockSpec(memory_space=pltpu.HBM)] * 2,
        out_specs=pl.BlockSpec(memory_space=pltpu.VMEM),
        scratch_shapes=[
            pltpu.VMEM((rows, depth), jnp.bfloat16),
            pltpu.VMEM((depth, eofs), jnp.bfloat16),
            pltpu.VMEM((half, eofs), jnp.float32),
            pltpu.VMEM((half, eofs), jnp.float32),
            pltpu.VMEM((half, eofs), jnp.float32),
            pltpu.VMEM((3, block, eofs), jnp.float32),
            pltpu.VMEM((lines, block, eofs), jnp.float32),
            dma((9,)), dma((2,)), dma((2,)), dma((3,)), dma((3,)), dma((lines,)), dma((lines,)),
            dma((3,)), dma((3,)), dma((4,)), dma((4,)),
        ],
        compiler_params=pltpu.CompilerParams(
            collective_id=0, has_side_effects=True, vmem_limit_bytes=VMEM_BYTES),
        cost_estimate=pl.CostEstimate(
            flops=2 * rows * depth * eofs, bytes_accessed=2 * depth * (rows + eofs), transcendentals=0),
    )(fields, basis)


def split(value, pieces):
    out = []
    for _ in range(pieces):
        part = value.astype(jnp.bfloat16)
        out.append(part)
        value = value - part.astype(jnp.float32)
    return out


def regime_kernel(seeds, amplitudes, fields, member_out, centers_out, composites, fbuf, load_sems):
    days, eofs = amplitudes.shape
    regimes = centers_out.shape[0]
    piece = days // CHUNKS
    loads = []
    for i in range(CHUNKS):
        load = pltpu.make_async_copy(fields.at[pl.ds(i * piece, piece)], fbuf.at[pl.ds(i * piece, piece)],
                                     load_sems.at[i])
        load.start()
        loads.append(load)

    turned = amplitudes[...].T
    with_ones = jnp.concatenate([turned, jnp.ones((8, days), jnp.float32)], axis=0)
    first, second, third = split(with_ones, 3)
    exact = jnp.concatenate([first, second, third], axis=1)
    five = jnp.concatenate([exact, first, second], axis=1)

    def member(columns):
        squares = []
        for c in range(regimes):
            offset = turned - columns[:, c:c + 1]
            squares.append(jnp.sum(offset * offset, axis=0, keepdims=True))
        mean_square = jnp.concatenate(squares, axis=0) * (1.0 / eofs) + 1e-05
        weights = 1.0 / mean_square
        return weights / jnp.sum(weights, axis=0, keepdims=True)

    positions = lax.broadcasted_iota(jnp.int32, (regimes, days), 1)
    rows = lax.broadcasted_iota(jnp.int32, (regimes, days), 0)
    chosen = jnp.zeros((regimes, days), jnp.int32)
    for c in range(regimes):
        chosen = jnp.where(rows == c, seeds[c], chosen)
    selector = (chosen == positions).astype(jnp.bfloat16)
    columns = lax.dot_general(exact, jnp.concatenate([selector] * 3, axis=1), NT,
                              preferred_element_type=jnp.float32)[:eofs]
    for sweep in range(ITERS):
        q = member(columns)
        high, low = split(q * q, 2)
        weights = jnp.concatenate([high, high, high, low, low], axis=1)
        sums = lax.dot_general(five, weights, NT, preferred_element_type=jnp.float32)
        columns = sums[:eofs] / sums[eofs:eofs + 1]
        if sweep == ITERS - 1:
            flat = lax.dot_general(weights, five, NT, preferred_element_type=jnp.float32)
            centers_out[...] = flat[:, :eofs] / flat[:, eofs:eofs + 1]
    final = member(columns)
    squares = final * final
    scale = 1.0 / jnp.sum(squares, axis=1, keepdims=True)
    weights_bf = squares.astype(jnp.bfloat16)
    member_out[...] = final
    for load in loads:
        load.wait()
    composites[...] = jnp.dot(weights_bf, fbuf[...], preferred_element_type=jnp.float32) * scale


def regimes_of(seed_days, amplitudes, fields):
    days, points = fields.shape
    eofs = amplitudes.shape[1]
    regimes = seed_days.shape[0]
    vmem = pl.BlockSpec(memory_space=pltpu.VMEM)
    member, centers, composites = pl.pallas_call(
        regime_kernel,
        out_shape=(
            jax.ShapeDtypeStruct((regimes, days), jnp.float32),
            jax.ShapeDtypeStruct((regimes, eofs), jnp.float32),
            jax.ShapeDtypeStruct((regimes, points), jnp.float32),
        ),
        in_specs=[pl.BlockSpec(memory_space=pltpu.SMEM), vmem, pl.BlockSpec(memory_space=pltpu.HBM)],
        out_specs=(vmem, vmem, vmem),
        scratch_shapes=[
            pltpu.VMEM((days, points), jnp.bfloat16),
            pltpu.SemaphoreType.DMA((CHUNKS,)),
        ],
        compiler_params=pltpu.CompilerParams(vmem_limit_bytes=VMEM_BYTES),
        cost_estimate=pl.CostEstimate(
            flops=2 * regimes * days * points, bytes_accessed=2 * days * points, transcendentals=0),
    )(seed_days, amplitudes, fields)
    return member.T, centers, composites


def on_device(mesh, fields, eof_basis, seed_days):
    n = mesh.shape["grid"]
    day_rows = fields.shape[0]
    if n % 8 == 0 and n > 8 and day_rows % 128 == 0:
        amplitudes = summed_amplitudes(n // 8, fields, eof_basis)
    else:
        partial_value = jnp.dot(fields, eof_basis, preferred_element_type=jnp.float32)
        amplitudes = lax.psum(partial_value, "grid")
    if mesh.shape["day"] == 1 and day_rows % 128 == 0 and eof_basis.shape[1] % 128 == 0:
        return regimes_of(seed_days, amplitudes, fields)
    first = lax.axis_index("day") * day_rows
    centers = lax.psum(seed_terms(seed_days, first, amplitudes), "day")
    for sweep in range(ITERS):
        numerator, denominator = lax.psum(regime_terms(amplitudes, centers), "day")
        centers = numerator / denominator[:, None]
    member_all = member_of(amplitudes, centers)
    squares = member_all * member_all
    weights_bf = squares.astype(jnp.bfloat16)
    weighted = jnp.dot(weights_bf.T, fields, preferred_element_type=jnp.float32)
    totals, weight_sums = lax.psum((weighted, jnp.sum(squares, axis=0)), "day")
    return (member_all, centers, totals / weight_sums[:, None])


def solution(mesh):
    placed = (P("day", "grid"), P("grid", None), P())
    return jax.shard_map(
        functools.partial(on_device, mesh),
        mesh=mesh,
        in_specs=placed,
        out_specs=(P("day", None), P(), P(None, "grid")),
        check_vma=False,
    )
```

time: 30.3 us -> 26.3 us (0.87)
  local copies, waits for them, and re-layouts: 4.56 us -> 0 us
  Pallas kernels: 24.9 us -> 25.5 us
    unnamed x4 -> x0, local copies, waits for them, and re-layouts: 3.11 us -> none
    reshape x1 -> x0, local copies, waits for them, and re-layouts: 0.73 us -> none  [regimes_of(): seed_days.reshape(regimes, 1)]
    pallas_call x1 -> x0, local copies, waits for them, and re-layouts: 0.71 us -> none  [regimes_of(): pl.pallas_call(regime_kernel, out_shape=(jax.ShapeDtypeStruct((days, regi...]
    pallas_call x2, Pallas kernels: 24.9 us -> 25.5 us  [the longest x1 19.7 us: summed_amplitudes(): pl.pallas_call(functools.partial(amplitude_kernel, lines), out_shape=jax....]
where the time goes in v2:
time: 26.3 us; the launch traced here: 26.2 us
  Pallas kernels  25.5 us (97%)
  between operations  0.64 us (2%)
    pallas_call x1, Pallas kernels, summed_amplitudes(): pl.pallas_call(functools.partial(amplitude_kernel, lines), out_shape=jax....  19.7 us
    pallas_call x1, Pallas kernels, regimes_of(): pl.pallas_call(regime_kernel, out_shape=(jax.ShapeDtypeStruct((regimes, d...  5.85 us

profile of v2, /device:TPU:0, one launch (start us, length us, event | category | flops | bytes accessed | tf_op | source)
XLA Modules:
  0.0 26.2 jit_solution(10069943407722363999)
XLA Ops:
  0.6 19.7 %shard_map.58.amplitudes = f32[384,128]{1,0:T(8,128)} custom-call(bf16[384,4096]{1,0:T(8,128)(2,1)} %fields.3, bf16[4096,128]{1,0:T(8,128)(2,1)} %basis.1), custom_call_target="tpu_custom_call" | custom-call | flops 402653184 | bytes 4194304 | tf_op jit(solution)/shard_map/pallas_call | solution.py:151
  20.3 5.9 %shard_map.59 = (f32[16,384]{1,0:T(8,128)}, f32[16,128]{1,0:T(8,128)}, f32[16,4096]{1,0:T(8,128)}) custom-call(s32[16]{0:T(128)} %seeds.1, f32[384,128]{1,0:T(8,128)} %shard_map.58.amplitudes, bf16[384,4096]{1,0:T(8,128)(2,1)} %fields.3), custom_call_target="tpu_custom_call" | custom-call | flops 50331648 | bytes 3145728 | tf_op jit(solution)/shard_map/pallas_call | solution.py:241

commit v3 on v2

--- a/solution.py
+++ b/solution.py
@@ -9,7 +9,8 @@
 
 ITERS = 3
 CHUNKS = 2
-VMEM_BYTES = 63 * 1024 * 1024 + 512 * 1024
+VMEM_BYTES = 53 * 1024 * 1024
+COLUMNS = 1024
 NT = (((1,), (1,)), ((), ()))
 
 
@@ -31,6 +32,10 @@
     squared = member * member
     numerator = jnp.dot(squared.T, amplitudes, precision=lax.Precision.HIGHEST)
     return (numerator, jnp.sum(squared, axis=0))
+
+
+def piece_sizes(block):
+    return [block - 16, 16] if block > 16 else [block]
 
 
 def amplitude_kernel(lines, fields, basis, out, fbuf, bbuf, give, take, mine, parts, stack, load_sems,
@@ -39,7 +44,6 @@
     rows = out.shape[0]
     half = rows // 2
     block = half // 4
-    piece = 2 * block
     me = lax.axis_index("grid")
     core = lax.rem(me, 2)
     spot = me // 2
@@ -56,90 +60,116 @@
     partner = me + 1 - 2 * core
     plane_peers = [(line * 4 + position) * 2 + core for position in order[:3]]
     line_steps = sorted(range(1, lines), key=lambda step: -min(step, lines - step))
-    line_peers = [lax.rem(line + step, lines) for step in line_steps]
-    line_devices = [(peer * 4 + plane) * 2 + core for peer in line_peers]
+    line_devices = [(lax.rem(line + step, lines) * 4 + plane) * 2 + core for step in line_steps]
+    line_sources = [lax.rem(line + lines - step, lines) for step in line_steps]
 
     barrier = pltpu.get_barrier_semaphore()
     for device in [partner] + plane_peers + line_devices:
         pl.semaphore_signal(barrier, inc=1, device_id={"grid": device}, device_id_type=pl.DeviceIdType.MESH)
 
-    basis_load = pltpu.make_async_copy(basis, bbuf, load_sems.at[8])
+    sizes = piece_sizes(block)
+    starts = [sum(sizes[:p]) for p in range(len(sizes))]
+    pieces = range(len(sizes))
+    basis_load = pltpu.make_async_copy(basis, bbuf, load_sems.at[0])
     basis_load.start()
-    loads = []
-    for i in range(8):
-        side = 1 - core if i < 4 else core
-        first = pl.multiple_of(side * half + order[i % 4] * block, 16)
-        load = pltpu.make_async_copy(fields.at[pl.ds(first, block)], fbuf.at[pl.ds(i * block, block)],
-                                     load_sems.at[i])
-        load.start()
-        loads.append(load)
+    loads = {}
+    for p in pieces:
+        for own in range(2):
+            for k in range(4):
+                side = core if own else 1 - core
+                first = pl.multiple_of(side * half + order[k] * block + starts[p], 16)
+                spot_in = own * half + 4 * starts[p] + k * sizes[p]
+                load = pltpu.make_async_copy(
+                    fields.at[pl.ds(first, sizes[p])], fbuf.at[pl.ds(spot_in, sizes[p])],
+                    load_sems.at[1 + (p * 2 + own) * 4 + k])
+                load.start()
+                loads[p, own, k] = load
     basis_load.wait()
 
-    def product(i):
-        loads[2 * i].wait()
-        loads[2 * i + 1].wait()
-        return jnp.dot(fbuf[i * piece:(i + 1) * piece, :], bbuf[...], preferred_element_type=jnp.float32)
+    def product(p, own):
+        for k in range(4):
+            loads[p, own, k].wait()
+        first = own * half + 4 * starts[p]
+        return jnp.dot(fbuf[first:first + 4 * sizes[p], :], bbuf[...], preferred_element_type=jnp.float32)
 
     started = []
-    pair_copies = []
-    for i in range(2):
-        part = pl.ds(i * piece, piece)
-        give[part, :] = product(i)
-        if i == 0:
-            pl.semaphore_wait(barrier, 1 + 3 + lines - 1)
-        copy = send(give.at[part], take.at[part], pair_send.at[i], pair_recv.at[i], partner)
-        copy.start()
-        pair_copies.append(copy)
-    plane_copies = []
-    for i in range(2):
-        part = pl.ds(i * piece, piece)
-        own = product(2 + i)
-        pair_copies[i].wait_recv()
-        mine[part, :] = own + take[part, :]
-        for k in (2 * i, 2 * i + 1):
-            if k < 3:
-                copy = send(mine.at[pl.ds(k * block, block)], parts.at[k], plane_send.at[k], plane_recv.at[k],
-                            plane_peers[k])
-                copy.start()
-                plane_copies.append(copy)
-    total = mine[3 * block:, :]
-    for k in (2, 1, 0):
-        plane_copies[k].wait_recv()
-        total = total + parts[k]
-    stack[line] = total
-
-    for step, device in enumerate(line_devices):
-        copy = send(stack.at[line], stack.at[line], line_send.at[step], line_recv.at[line], device)
+
+    def begin(*what):
+        copy = send(*what)
         copy.start()
         started.append(copy)
-    for step in range(lines - 1):
-        source = lax.rem(line + lines - line_steps[step], lines)
-        send(stack.at[source], stack.at[source], line_send.at[step], line_recv.at[source],
-             (source * 4 + plane) * 2 + core).wait_recv()
-    total = stack[0]
-    for j in range(1, lines):
-        total = total + stack[j]
-
-    def place(side, position):
-        return out.at[pl.ds(pl.multiple_of(side * half + position * block, 8), block)]
-
-    place(core, plane)[...] = total
-    back_copies = []
-    for k in range(3):
-        copy = send(place(core, plane), place(core, plane), back_send.at[k], back_recv.at[k], plane_peers[k])
-        copy.start()
-        back_copies.append(copy)
-    for k in (3, 2, 1, 0):
-        if k < 3:
-            send(place(core, order[k]), place(core, order[k]), back_send.at[k], back_recv.at[k],
+        return copy
+
+    def span(p):
+        return pl.ds(4 * starts[p], 4 * sizes[p])
+
+    pair_copies, plane_copies = [], {}
+
+    def give_piece(p):
+        give[span(p), :] = product(p, 0)
+        if p == 0:
+            pl.semaphore_wait(barrier, 1 + 3 + lines - 1)
+        pair_copies.append(begin(give.at[span(p)], take.at[span(p)], pair_send.at[p], pair_recv.at[p], partner))
+
+    def spread_piece(p):
+        pair_copies[p].wait_recv()
+        mine[span(p), :] = mine[span(p), :] + take[span(p), :]
+        for k in range(3):
+            plane_copies[p, k] = begin(
+                mine.at[pl.ds(4 * starts[p] + k * sizes[p], sizes[p])], parts.at[k, pl.ds(starts[p], sizes[p])],
+                plane_send.at[p * 3 + k], plane_recv.at[p * 3 + k], plane_peers[k])
+
+    give_piece(0)
+    mine[span(0), :] = product(0, 1)
+    for p in pieces[1:]:
+        give_piece(p)
+        spread_piece(p - 1)
+        mine[span(p), :] = product(p, 1)
+    spread_piece(pieces[-1])
+
+    def rows_of(p):
+        return pl.ds(starts[p], sizes[p])
+
+    for p in pieces:
+        first = 4 * starts[p] + 3 * sizes[p]
+        total = mine[first:first + sizes[p], :]
+        for k in (2, 1, 0):
+            plane_copies[p, k].wait_recv()
+            total = total + parts[k, rows_of(p), :]
+        stack[line, rows_of(p), :] = total
+        for step, device in enumerate(line_devices):
+            slot = stack.at[line, rows_of(p)]
+            begin(slot, slot, line_send.at[p * lines + step], line_recv.at[p * lines + line], device)
+
+    def place(side, k, p):
+        return out.at[pl.ds(pl.multiple_of(side * half + order[k] * block + starts[p], 8), sizes[p])]
+
+    def forward(k, p):
+        begin(place(core, k, p), place(core, k, p), final_send.at[p * 4 + k], final_recv.at[p * 4 + k], partner)
+
+    for p in pieces:
+        for step, source in enumerate(line_sources):
+            slot = stack.at[source, rows_of(p)]
+            send(slot, slot, line_send.at[p * lines + step], line_recv.at[p * lines + source],
+                 (source * 4 + plane) * 2 + core).wait_recv()
+        total = stack[0, rows_of(p), :]
+        for j in range(1, lines):
+            total = total + stack[j, rows_of(p), :]
+        place(core, 3, p)[...] = total
+        for k in range(3):
+            begin(place(core, 3, p), place(core, 3, p), back_send.at[p * 3 + k], back_recv.at[p * 3 + k],
+                  plane_peers[k])
+        forward(3, p)
+    for p in pieces:
+        for k in (2, 1, 0):
+            send(place(core, k, p), place(core, k, p), back_send.at[p * 3 + k], back_recv.at[p * 3 + k],
                  plane_peers[k]).wait_recv()
-        copy = send(place(core, order[k]), place(core, order[k]), final_send.at[k], final_recv.at[k], partner)
-        copy.start()
-        started.append(copy)
-    for k in (3, 2, 1, 0):
-        send(place(1 - core, order[k]), place(1 - core, order[k]), final_send.at[k], final_recv.at[k],
-             partner).wait_recv()
-    for copy in pair_copies + plane_copies + started + back_copies:
+            forward(k, p)
+    for p in pieces:
+        for k in (3, 2, 1, 0):
+            send(place(1 - core, k, p), place(1 - core, k, p), final_send.at[p * 4 + k],
+                 final_recv.at[p * 4 + k], partner).wait_recv()
+    for copy in started:
         copy.wait_send()
 
 
@@ -147,6 +177,7 @@
     rows, depth = fields.shape
     eofs = basis.shape[1]
     half, block = rows // 2, rows // 8
+    pieces = len(piece_sizes(block))
     dma = pltpu.SemaphoreType.DMA
     return pl.pallas_call(
         functools.partial(amplitude_kernel, lines),
@@ -161,8 +192,9 @@
             pltpu.VMEM((half, eofs), jnp.float32),
             pltpu.VMEM((3, block, eofs), jnp.float32),
             pltpu.VMEM((lines, block, eofs), jnp.float32),
-            dma((9,)), dma((2,)), dma((2,)), dma((3,)), dma((3,)), dma((lines,)), dma((lines,)),
-            dma((3,)), dma((3,)), dma((4,)), dma((4,)),
+            dma((1 + 8 * pieces,)), dma((pieces,)), dma((pieces,)), dma((3 * pieces,)), dma((3 * pieces,)),
+            dma((lines * pieces,)), dma((lines * pieces,)), dma((3 * pieces,)), dma((3 * pieces,)),
+            dma((4 * pieces,)), dma((4 * pieces,)),
         ],
         compiler_params=pltpu.CompilerParams(
             collective_id=0, has_side_effects=True, vmem_limit_bytes=VMEM_BYTES),
@@ -180,9 +212,10 @@
     return out
 
 
-def regime_kernel(seeds, amplitudes, fields, member_out, centers_out, composites, fbuf, load_sems):
+def regime_kernel(seeds, amplitudes, fields, member_out, centers_out, composites, fbuf, member_buf, centers_buf,
+                  composite_buf, load_sems, store_sems):
     days, eofs = amplitudes.shape
-    regimes = centers_out.shape[0]
+    regimes, points = composites.shape
     piece = days // CHUNKS
     loads = []
     for i in range(CHUNKS):
@@ -192,10 +225,16 @@
         loads.append(load)
 
     turned = amplitudes[...].T
-    with_ones = jnp.concatenate([turned, jnp.ones((8, days), jnp.float32)], axis=0)
+    with_ones = jnp.concatenate([turned, jnp.ones((16, days), jnp.float32)], axis=0)
     first, second, third = split(with_ones, 3)
     exact = jnp.concatenate([first, second, third], axis=1)
-    five = jnp.concatenate([exact, first, second], axis=1)
+    pair = jnp.concatenate([first, second, first], axis=1)
+    stores = []
+
+    def store(src, dst):
+        copy = pltpu.make_async_copy(src, dst, store_sems.at[len(stores)])
+        copy.start()
+        stores.append(copy)
 
     def member(columns):
         squares = []
@@ -217,20 +256,29 @@
     for sweep in range(ITERS):
         q = member(columns)
         high, low = split(q * q, 2)
-        weights = jnp.concatenate([high, high, high, low, low], axis=1)
-        sums = lax.dot_general(five, weights, NT, preferred_element_type=jnp.float32)
+        weights = jnp.concatenate([high, high, low], axis=1)
+        sums = lax.dot_general(pair, weights, NT, preferred_element_type=jnp.float32)
         columns = sums[:eofs] / sums[eofs:eofs + 1]
         if sweep == ITERS - 1:
-            flat = lax.dot_general(weights, five, NT, preferred_element_type=jnp.float32)
-            centers_out[...] = flat[:, :eofs] / flat[:, eofs:eofs + 1]
+            flat = lax.dot_general(weights, pair, NT, preferred_element_type=jnp.float32)
+            centers_buf[...] = flat[:, :eofs] / flat[:, eofs:eofs + 1]
+            store(centers_buf, centers_out)
     final = member(columns)
     squares = final * final
     scale = 1.0 / jnp.sum(squares, axis=1, keepdims=True)
     weights_bf = squares.astype(jnp.bfloat16)
-    member_out[...] = final
+    member_buf[...] = final
+    store(member_buf, member_out)
     for load in loads:
         load.wait()
-    composites[...] = jnp.dot(weights_bf, fbuf[...], preferred_element_type=jnp.float32) * scale
+    width = COLUMNS if points % COLUMNS == 0 else points
+    for first in range(0, points, width):
+        part = slice(first, first + width)
+        composite_buf[:, part] = jnp.dot(
+            weights_bf, fbuf[:, part], preferred_element_type=jnp.float32) * scale
+        store(composite_buf.at[:, pl.ds(first, width)], composites.at[:, pl.ds(first, width)])
+    for copy in stores:
+        copy.wait()
 
 
 def regimes_of(seed_days, amplitudes, fields):
@@ -238,6 +286,7 @@
     eofs = amplitudes.shape[1]
     regimes = seed_days.shape[0]
     vmem = pl.BlockSpec(memory_space=pltpu.VMEM)
+    hbm = pl.BlockSpec(memory_space=pltpu.HBM)
     member, centers, composites = pl.pallas_call(
         regime_kernel,
         out_shape=(
@@ -245,11 +294,15 @@
             jax.ShapeDtypeStruct((regimes, eofs), jnp.float32),
             jax.ShapeDtypeStruct((regimes, points), jnp.float32),
         ),
-        in_specs=[pl.BlockSpec(memory_space=pltpu.SMEM), vmem, pl.BlockSpec(memory_space=pltpu.HBM)],
-        out_specs=(vmem, vmem, vmem),
+        in_specs=[pl.BlockSpec(memory_space=pltpu.SMEM), vmem, hbm],
+        out_specs=(hbm, hbm, hbm),
         scratch_shapes=[
             pltpu.VMEM((days, points), jnp.bfloat16),
+            pltpu.VMEM((regimes, days), jnp.float32),
+            pltpu.VMEM((regimes, eofs), jnp.float32),
+            pltpu.VMEM((regimes, points), jnp.float32),
             pltpu.SemaphoreType.DMA((CHUNKS,)),
+            pltpu.SemaphoreType.DMA((2 + max(1, points // COLUMNS),)),
         ],
         compiler_params=pltpu.CompilerParams(vmem_limit_bytes=VMEM_BYTES),
         cost_estimate=pl.CostEstimate(

time: 26.3 us -> 24.4 us (0.928)
  Pallas kernels: 25.5 us -> 23.6 us
    pallas_call x1, Pallas kernels: 19.7 us -> 18.5 us  [summed_amplitudes(): pl.pallas_call(functools.partial(amplitude_kernel, lines), out_shape=jax....]
    pallas_call x1, Pallas kernels: 5.85 us -> 5.1 us  [regimes_of(): pl.pallas_call(regime_kernel, out_shape=(jax.ShapeDtypeStruct((regimes, d...]
where the time goes in v3:
time: 24.4 us; the launch traced here: 24.3 us
  Pallas kernels  23.6 us (97%)
  between operations  0.65 us (3%)
    pallas_call x1, Pallas kernels, summed_amplitudes(): pl.pallas_call(functools.partial(amplitude_kernel, lines), out_shape=jax....  18.5 us
    pallas_call x1, Pallas kernels, regimes_of(): pl.pallas_call(regime_kernel, out_shape=(jax.ShapeDtypeStruct((regimes, d...  5.1 us

profile of v3, /device:TPU:0, one launch (start us, length us, event | category | flops | bytes accessed | tf_op | source)
XLA Modules:
  0.0 24.3 jit_solution(1648050600046844675)
XLA Ops:
  0.6 0.0 copy-start
  0.6 18.5 %shard_map.58.amplitudes = f32[384,128]{1,0:T(8,128)S(1)} custom-call(bf16[384,4096]{1,0:T(8,128)(2,1)} %fields.3, bf16[4096,128]{1,0:T(8,128)(2,1)} %basis.1), custom_call_target="tpu_custom_call" | custom-call | flops 402653184 | bytes 4194304 | tf_op jit(solution)/shard_map/pallas_call | solution.py:182
  19.2 0.0 copy-done
  19.2 5.1 %shard_map.59 = (f32[16,384]{1,0:T(8,128)}, f32[16,128]{1,0:T(8,128)}, f32[16,4096]{1,0:T(8,128)}) custom-call(s32[16]{0:T(128)S(1)} %copy-done, f32[384,128]{1,0:T(8,128)S(1)} %shard_map.58.amplitudes, bf16[384,4096]{1,0:T(8,128)(2,1)} %fields.3), custom_call_target="tpu_custom_call" | custom-call | flops 50331648 | bytes 3145728 | tf_op jit(solution)/shard_map/pallas_call | solution.py:290
Async XLA Ops:
  0.6 18.6 %copy-start = (s32[16]{0:T(128)S(1)}, s32[16]{0:T(128)}, u32[]{:S(2)}) copy-start(s32[16]{0:T(128)} %seeds.1) | copy-start | bytes 196

commit v4 on v3

--- a/solution.py
+++ b/solution.py
@@ -35,36 +35,39 @@
 
 
 def piece_sizes(block):
-    return [block - 16, 16] if block > 16 else [block]
-
-
-def amplitude_kernel(lines, fields, basis, out, fbuf, bbuf, give, take, mine, parts, stack, load_sems,
-                     pair_send, pair_recv, plane_send, plane_recv, line_send, line_recv,
-                     back_send, back_recv, final_send, final_recv):
+    return [16] * (block // 16)
+
+
+def amplitude_kernel(lines, fields, basis, out, fbuf, bbuf, mine, parts, stack, load_sems,
+                     plane_send, plane_recv, line_send, line_recv, back_send, back_recv):
     rows = out.shape[0]
-    half = rows // 2
-    block = half // 4
+    block = rows // 8
     me = lax.axis_index("grid")
     core = lax.rem(me, 2)
-    spot = me // 2
-    plane = lax.rem(spot, 4)
-    line = spot // 4
-    px, py = lax.rem(plane, 2), plane // 2
-    order = [(1 - py) * 2 + 1 - px, (1 - py) * 2 + px, py * 2 + 1 - px, plane]
+    px = lax.rem(me // 2, 2)
+    py = lax.rem(me // 4, 2)
+    line = me // 8
+    flips = [(1, 1, 0), (1, 1, 1), (1, 0, 0), (1, 0, 1), (0, 1, 0), (0, 1, 1), (0, 0, 1), (0, 0, 0)]
+    order = []
+    for fy, fx, fc in flips:
+        y = 1 - py if fy else py
+        x = 1 - px if fx else px
+        c = 1 - core if fc else core
+        order.append((y * 2 + x) * 2 + c)
+    own = order[7]
 
     def send(src, dst, send_sem, recv_sem, device):
         return pltpu.make_async_remote_copy(
             src_ref=src, dst_ref=dst, send_sem=send_sem, recv_sem=recv_sem,
             device_id={"grid": device}, device_id_type=pl.DeviceIdType.MESH)
 
-    partner = me + 1 - 2 * core
-    plane_peers = [(line * 4 + position) * 2 + core for position in order[:3]]
+    plane_peers = [line * 8 + position for position in order[:7]]
     line_steps = sorted(range(1, lines), key=lambda step: -min(step, lines - step))
-    line_devices = [(lax.rem(line + step, lines) * 4 + plane) * 2 + core for step in line_steps]
+    line_devices = [lax.rem(line + step, lines) * 8 + own for step in line_steps]
     line_sources = [lax.rem(line + lines - step, lines) for step in line_steps]
 
     barrier = pltpu.get_barrier_semaphore()
-    for device in [partner] + plane_peers + line_devices:
+    for device in line_devices + plane_peers:
         pl.semaphore_signal(barrier, inc=1, device_id={"grid": device}, device_id_type=pl.DeviceIdType.MESH)
 
     sizes = piece_sizes(block)
@@ -74,23 +77,13 @@
     basis_load.start()
     loads = {}
     for p in pieces:
-        for own in range(2):
-            for k in range(4):
-                side = core if own else 1 - core
-                first = pl.multiple_of(side * half + order[k] * block + starts[p], 16)
-                spot_in = own * half + 4 * starts[p] + k * sizes[p]
-                load = pltpu.make_async_copy(
-                    fields.at[pl.ds(first, sizes[p])], fbuf.at[pl.ds(spot_in, sizes[p])],
-                    load_sems.at[1 + (p * 2 + own) * 4 + k])
-                load.start()
-                loads[p, own, k] = load
-    basis_load.wait()
-
-    def product(p, own):
-        for k in range(4):
-            loads[p, own, k].wait()
-        first = own * half + 4 * starts[p]
-        return jnp.dot(fbuf[first:first + 4 * sizes[p], :], bbuf[...], preferred_element_type=jnp.float32)
+        for k in range(8):
+            first = pl.multiple_of(order[k] * block + starts[p], 16)
+            load = pltpu.make_async_copy(
+                fields.at[pl.ds(first, sizes[p])], fbuf.at[pl.ds(8 * starts[p] + k * sizes[p], sizes[p])],
+                load_sems.at[1 + p * 8 + k])
+            load.start()
+            loads[p, k] = load
 
     started = []
 
@@ -100,75 +93,52 @@
         started.append(copy)
         return copy
 
-    def span(p):
-        return pl.ds(4 * starts[p], 4 * sizes[p])
-
-    pair_copies, plane_copies = [], {}
-
-    def give_piece(p):
-        give[span(p), :] = product(p, 0)
-        if p == 0:
-            pl.semaphore_wait(barrier, 1 + 3 + lines - 1)
-        pair_copies.append(begin(give.at[span(p)], take.at[span(p)], pair_send.at[p], pair_recv.at[p], partner))
-
-    def spread_piece(p):
-        pair_copies[p].wait_recv()
-        mine[span(p), :] = mine[span(p), :] + take[span(p), :]
-        for k in range(3):
-            plane_copies[p, k] = begin(
-                mine.at[pl.ds(4 * starts[p] + k * sizes[p], sizes[p])], parts.at[k, pl.ds(starts[p], sizes[p])],
-                plane_send.at[p * 3 + k], plane_recv.at[p * 3 + k], plane_peers[k])
-
-    give_piece(0)
-    mine[span(0), :] = product(0, 1)
-    for p in pieces[1:]:
-        give_piece(p)
-        spread_piece(p - 1)
-        mine[span(p), :] = product(p, 1)
-    spread_piece(pieces[-1])
-
     def rows_of(p):
         return pl.ds(starts[p], sizes[p])
 
-    for p in pieces:
-        first = 4 * starts[p] + 3 * sizes[p]
+    basis_load.wait()
+    plane_copies = {}
+    for p in pieces:
+        for k in range(8):
+            loads[p, k].wait()
+        span = slice(8 * starts[p], 8 * (starts[p] + sizes[p]))
+        mine[span, :] = jnp.dot(fbuf[span, :], bbuf[...], preferred_element_type=jnp.float32)
+        if p == 0:
+            pl.semaphore_wait(barrier, 7 + lines - 1)
+        for k in range(7):
+            plane_copies[p, k] = begin(
+                mine.at[pl.ds(8 * starts[p] + k * sizes[p], sizes[p])], parts.at[k, rows_of(p)],
+                plane_send.at[p * 7 + k], plane_recv.at[p * 7 + k], plane_peers[k])
+
+    for p in pieces:
+        first = 8 * starts[p] + 7 * sizes[p]
         total = mine[first:first + sizes[p], :]
-        for k in (2, 1, 0):
+        for k in reversed(range(7)):
             plane_copies[p, k].wait_recv()
             total = total + parts[k, rows_of(p), :]
         stack[line, rows_of(p), :] = total
+        slot = stack.at[line, rows_of(p)]
         for step, device in enumerate(line_devices):
-            slot = stack.at[line, rows_of(p)]
             begin(slot, slot, line_send.at[p * lines + step], line_recv.at[p * lines + line], device)
 
-    def place(side, k, p):
-        return out.at[pl.ds(pl.multiple_of(side * half + order[k] * block + starts[p], 8), sizes[p])]
-
-    def forward(k, p):
-        begin(place(core, k, p), place(core, k, p), final_send.at[p * 4 + k], final_recv.at[p * 4 + k], partner)
+    def place(k, p):
+        return out.at[pl.ds(pl.multiple_of(order[k] * block + starts[p], 8), sizes[p])]
 
     for p in pieces:
         for step, source in enumerate(line_sources):
             slot = stack.at[source, rows_of(p)]
             send(slot, slot, line_send.at[p * lines + step], line_recv.at[p * lines + source],
-                 (source * 4 + plane) * 2 + core).wait_recv()
+                 source * 8 + own).wait_recv()
         total = stack[0, rows_of(p), :]
         for j in range(1, lines):
             total = total + stack[j, rows_of(p), :]
-        place(core, 3, p)[...] = total
-        for k in range(3):
-            begin(place(core, 3, p), place(core, 3, p), back_send.at[p * 3 + k], back_recv.at[p * 3 + k],
-                  plane_peers[k])
-        forward(3, p)
-    for p in pieces:
-        for k in (2, 1, 0):
-            send(place(core, k, p), place(core, k, p), back_send.at[p * 3 + k], back_recv.at[p * 3 + k],
+        place(7, p)[...] = total
+        for k in range(7):
+            begin(place(7, p), place(7, p), back_send.at[p * 7 + k], back_recv.at[p * 7 + k], plane_peers[k])
+    for p in pieces:
+        for k in reversed(range(7)):
+            send(place(k, p), place(k, p), back_send.at[p * 7 + k], back_recv.at[p * 7 + k],
                  plane_peers[k]).wait_recv()
-            forward(k, p)
-    for p in pieces:
-        for k in (3, 2, 1, 0):
-            send(place(1 - core, k, p), place(1 - core, k, p), final_send.at[p * 4 + k],
-                 final_recv.at[p * 4 + k], partner).wait_recv()
     for copy in started:
         copy.wait_send()
 
@@ -176,7 +146,7 @@
 def summed_amplitudes(lines, fields, basis):
     rows, depth = fields.shape
     eofs = basis.shape[1]
-    half, block = rows // 2, rows // 8
+    block = rows // 8
     pieces = len(piece_sizes(block))
     dma = pltpu.SemaphoreType.DMA
     return pl.pallas_call(
@@ -187,14 +157,11 @@
         scratch_shapes=[
             pltpu.VMEM((rows, depth), jnp.bfloat16),
             pltpu.VMEM((depth, eofs), jnp.bfloat16),
-            pltpu.VMEM((half, eofs), jnp.float32),
-            pltpu.VMEM((half, eofs), jnp.float32),
-            pltpu.VMEM((half, eofs), jnp.float32),
-            pltpu.VMEM((3, block, eofs), jnp.float32),
+            pltpu.VMEM((rows, eofs), jnp.float32),
+            pltpu.VMEM((7, block, eofs), jnp.float32),
             pltpu.VMEM((lines, block, eofs), jnp.float32),
-            dma((1 + 8 * pieces,)), dma((pieces,)), dma((pieces,)), dma((3 * pieces,)), dma((3 * pieces,)),
-            dma((lines * pieces,)), dma((lines * pieces,)), dma((3 * pieces,)), dma((3 * pieces,)),
-            dma((4 * pieces,)), dma((4 * pieces,)),
+            dma((1 + 8 * pieces,)), dma((7 * pieces,)), dma((7 * pieces,)),
+            dma((lines * pieces,)), dma((lines * pieces,)), dma((7 * pieces,)), dma((7 * pieces,)),
         ],
         compiler_params=pltpu.CompilerParams(
             collective_id=0, has_side_effects=True, vmem_limit_bytes=VMEM_BYTES),

time: 24.4 us -> 23.9 us (0.980)
  Pallas kernels: 23.6 us -> 23.1 us
    pallas_call x1, Pallas kernels: 18.5 us -> 18 us  [summed_amplitudes(): pl.pallas_call(functools.partial(amplitude_kernel, lines), out_shape=jax....]
where the time goes in v4:
time: 23.9 us; the launch traced here: 23.8 us
  Pallas kernels  23.1 us (97%)
  between operations  0.65 us (3%)
    pallas_call x1, Pallas kernels, summed_amplitudes(): pl.pallas_call(functools.partial(amplitude_kernel, lines), out_shape=jax....  18 us
    pallas_call x1, Pallas kernels, regimes_of(): pl.pallas_call(regime_kernel, out_shape=(jax.ShapeDtypeStruct((regimes, d...  5.1 us

profile of v4, /device:TPU:0, one launch (start us, length us, event | category | flops | bytes accessed | tf_op | source)
XLA Modules:
  0.0 23.8 jit_solution(8291014085512501169)
XLA Ops:
  0.6 0.0 copy-start
  0.6 18.0 %shard_map.58.amplitudes = f32[384,128]{1,0:T(8,128)S(1)} custom-call(bf16[384,4096]{1,0:T(8,128)(2,1)} %fields.3, bf16[4096,128]{1,0:T(8,128)(2,1)} %basis.1), custom_call_target="tpu_custom_call" | custom-call | flops 402653184 | bytes 4194304 | tf_op jit(solution)/shard_map/pallas_call | solution.py:152
  18.7 0.0 copy-done
  18.7 5.1 %shard_map.59 = (f32[16,384]{1,0:T(8,128)}, f32[16,128]{1,0:T(8,128)}, f32[16,4096]{1,0:T(8,128)}) custom-call(s32[16]{0:T(128)S(1)} %copy-done, f32[384,128]{1,0:T(8,128)S(1)} %shard_map.58.amplitudes, bf16[384,4096]{1,0:T(8,128)(2,1)} %fields.3), custom_call_target="tpu_custom_call" | custom-call | flops 50331648 | bytes 3145728 | tf_op jit(solution)/shard_map/pallas_call | solution.py:257
Async XLA Ops:
  0.6 18.1 %copy-start = (s32[16]{0:T(128)S(1)}, s32[16]{0:T(128)}, u32[]{:S(2)}) copy-start(s32[16]{0:T(128)} %seeds.1) | copy-start | bytes 196

commit v5 on v4

--- a/solution.py
+++ b/solution.py
@@ -11,6 +11,7 @@
 CHUNKS = 2
 VMEM_BYTES = 53 * 1024 * 1024
 COLUMNS = 1024
+BASIS_COPIES = 4
 NT = (((1,), (1,)), ((), ()))
 
 
@@ -38,8 +39,8 @@
     return [16] * (block // 16)
 
 
-def amplitude_kernel(lines, fields, basis, out, fbuf, bbuf, mine, parts, stack, load_sems,
-                     plane_send, plane_recv, line_send, line_recv, back_send, back_recv):
+def amplitude_kernel(lines, fields, basis, out, fbuf, bbuf, mine, take, parts, stack, load_sems,
+                     pair_send, pair_recv, plane_send, plane_recv, line_send, line_recv, back_send, back_recv):
     rows = out.shape[0]
     block = rows // 8
     me = lax.axis_index("grid")
@@ -47,7 +48,7 @@
     px = lax.rem(me // 2, 2)
     py = lax.rem(me // 4, 2)
     line = me // 8
-    flips = [(1, 1, 0), (1, 1, 1), (1, 0, 0), (1, 0, 1), (0, 1, 0), (0, 1, 1), (0, 0, 1), (0, 0, 0)]
+    flips = [(1, 1, 1), (1, 0, 1), (0, 1, 1), (0, 0, 1), (1, 1, 0), (1, 0, 0), (0, 1, 0), (0, 0, 0)]
     order = []
     for fy, fx, fc in flips:
         y = 1 - py if fy else py
@@ -73,15 +74,20 @@
     sizes = piece_sizes(block)
     starts = [sum(sizes[:p]) for p in range(len(sizes))]
     pieces = range(len(sizes))
-    basis_load = pltpu.make_async_copy(basis, bbuf, load_sems.at[0])
-    basis_load.start()
+    depth = basis.shape[0] // BASIS_COPIES
+    basis_loads = []
+    for i in range(BASIS_COPIES):
+        part = pl.ds(i * depth, depth)
+        load = pltpu.make_async_copy(basis.at[part], bbuf.at[part], load_sems.at[i])
+        load.start()
+        basis_loads.append(load)
     loads = {}
     for p in pieces:
         for k in range(8):
             first = pl.multiple_of(order[k] * block + starts[p], 16)
             load = pltpu.make_async_copy(
                 fields.at[pl.ds(first, sizes[p])], fbuf.at[pl.ds(8 * starts[p] + k * sizes[p], sizes[p])],
-                load_sems.at[1 + p * 8 + k])
+                load_sems.at[BASIS_COPIES + p * 8 + k])
             load.start()
             loads[p, k] = load
 
@@ -96,8 +102,20 @@
     def rows_of(p):
         return pl.ds(starts[p], sizes[p])
 
-    basis_load.wait()
-    plane_copies = {}
+    for load in basis_loads:
+        load.wait()
+    pair_copies, plane_copies = [], {}
+
+    def spread_piece(p):
+        first = 8 * starts[p] + 4 * sizes[p]
+        pair_copies[p].wait_recv()
+        mine[first:first + 4 * sizes[p], :] = (
+            mine[first:first + 4 * sizes[p], :] + take[4 * starts[p]:4 * (starts[p] + sizes[p]), :])
+        for k in range(3):
+            plane_copies[p, k] = begin(
+                mine.at[pl.ds(first + k * sizes[p], sizes[p])], parts.at[k, rows_of(p)],
+                plane_send.at[p * 3 + k], plane_recv.at[p * 3 + k], plane_peers[4 + k])
+
     for p in pieces:
         for k in range(8):
             loads[p, k].wait()
@@ -105,21 +123,25 @@
         mine[span, :] = jnp.dot(fbuf[span, :], bbuf[...], preferred_element_type=jnp.float32)
         if p == 0:
             pl.semaphore_wait(barrier, 7 + lines - 1)
-        for k in range(7):
-            plane_copies[p, k] = begin(
-                mine.at[pl.ds(8 * starts[p] + k * sizes[p], sizes[p])], parts.at[k, rows_of(p)],
-                plane_send.at[p * 7 + k], plane_recv.at[p * 7 + k], plane_peers[k])
+        pair_copies.append(begin(
+            mine.at[pl.ds(8 * starts[p], 4 * sizes[p])], take.at[pl.ds(4 * starts[p], 4 * sizes[p])],
+            pair_send.at[p], pair_recv.at[p], plane_peers[3]))
+        if p > 0:
+            spread_piece(p - 1)
+    spread_piece(pieces[-1])
 
     for p in pieces:
         first = 8 * starts[p] + 7 * sizes[p]
         total = mine[first:first + sizes[p], :]
-        for k in reversed(range(7)):
+        for k in (2, 1, 0):
             plane_copies[p, k].wait_recv()
             total = total + parts[k, rows_of(p), :]
         stack[line, rows_of(p), :] = total
         slot = stack.at[line, rows_of(p)]
         for step, device in enumerate(line_devices):
             begin(slot, slot, line_send.at[p * lines + step], line_recv.at[p * lines + line], device)
+
+    back_order = (0, 4, 1, 5, 2, 6, 3)
 
     def place(k, p):
         return out.at[pl.ds(pl.multiple_of(order[k] * block + starts[p], 8), sizes[p])]
@@ -133,10 +155,10 @@
         for j in range(1, lines):
             total = total + stack[j, rows_of(p), :]
         place(7, p)[...] = total
-        for k in range(7):
+        for k in back_order:
             begin(place(7, p), place(7, p), back_send.at[p * 7 + k], back_recv.at[p * 7 + k], plane_peers[k])
     for p in pieces:
-        for k in reversed(range(7)):
+        for k in reversed(back_order):
             send(place(k, p), place(k, p), back_send.at[p * 7 + k], back_recv.at[p * 7 + k],
                  plane_peers[k]).wait_recv()
     for copy in started:
@@ -158,9 +180,10 @@
             pltpu.VMEM((rows, depth), jnp.bfloat16),
             pltpu.VMEM((depth, eofs), jnp.bfloat16),
             pltpu.VMEM((rows, eofs), jnp.float32),
-            pltpu.VMEM((7, block, eofs), jnp.float32),
+            pltpu.VMEM((rows // 2, eofs), jnp.float32),
+            pltpu.VMEM((3, block, eofs), jnp.float32),
             pltpu.VMEM((lines, block, eofs), jnp.float32),
-            dma((1 + 8 * pieces,)), dma((7 * pieces,)), dma((7 * pieces,)),
+            dma((BASIS_COPIES + 8 * pieces,)), dma((pieces,)), dma((pieces,)), dma((3 * pieces,)), dma((3 * pieces,)),
             dma((lines * pieces,)), dma((lines * pieces,)), dma((7 * pieces,)), dma((7 * pieces,)),
         ],
         compiler_params=pltpu.CompilerParams(
@@ -281,7 +304,7 @@
 def on_device(mesh, fields, eof_basis, seed_days):
     n = mesh.shape["grid"]
     day_rows = fields.shape[0]
-    if n % 8 == 0 and n > 8 and day_rows % 128 == 0:
+    if n % 8 == 0 and n > 8 and day_rows % 128 == 0 and eof_basis.shape[0] % (16 * BASIS_COPIES) == 0:
         amplitudes = summed_amplitudes(n // 8, fields, eof_basis)
     else:
         partial_value = jnp.dot(fields, eof_basis, preferred_element_type=jnp.float32)

time: 23.9 us -> 24.9 us (1.042)
  Pallas kernels: 23.1 us -> 24.1 us
    pallas_call x1, Pallas kernels: 18 us -> 19 us  [summed_amplitudes(): pl.pallas_call(functools.partial(amplitude_kernel, lines), out_shape=jax....]
where the time goes in v5:
time: 24.9 us; the launch traced here: 24.8 us
  Pallas kernels  24.1 us (97%)
  between operations  0.65 us (3%)
    pallas_call x1, Pallas kernels, summed_amplitudes(): pl.pallas_call(functools.partial(amplitude_kernel, lines), out_shape=jax....  19 us
    pallas_call x1, Pallas kernels, regimes_of(): pl.pallas_call(regime_kernel, out_shape=(jax.ShapeDtypeStruct((regimes, d...  5.1 us

profile of v5, /device:TPU:0, one launch (start us, length us, event | category | flops | bytes accessed | tf_op | source)
XLA Modules:
  0.0 24.8 jit_solution(7415835914868163911)
XLA Ops:
  0.6 0.0 copy-start
  0.6 19.0 %shard_map.58.amplitudes = f32[384,128]{1,0:T(8,128)S(1)} custom-call(bf16[384,4096]{1,0:T(8,128)(2,1)} %fields.3, bf16[4096,128]{1,0:T(8,128)(2,1)} %basis.1), custom_call_target="tpu_custom_call" | custom-call | flops 402653184 | bytes 4194304 | tf_op jit(solution)/shard_map/pallas_call | solution.py:174
  19.7 0.0 copy-done
  19.7 5.1 %shard_map.59 = (f32[16,384]{1,0:T(8,128)}, f32[16,128]{1,0:T(8,128)}, f32[16,4096]{1,0:T(8,128)}) custom-call(s32[16]{0:T(128)S(1)} %copy-done, f32[384,128]{1,0:T(8,128)S(1)} %shard_map.58.amplitudes, bf16[384,4096]{1,0:T(8,128)(2,1)} %fields.3), custom_call_target="tpu_custom_call" | custom-call | flops 50331648 | bytes 3145728 | tf_op jit(solution)/shard_map/pallas_call | solution.py:280
Async XLA Ops:
  0.6 19.1 %copy-start = (s32[16]{0:T(128)S(1)}, s32[16]{0:T(128)}, u32[]{:S(2)}) copy-start(s32[16]{0:T(128)} %seeds.1) | copy-start | bytes 196

commit v6 on v4

--- a/solution.py
+++ b/solution.py
@@ -35,7 +35,7 @@
 
 
 def piece_sizes(block):
-    return [16] * (block // 16)
+    return [block - 16, 16] if block > 16 else [block]
 
 
 def amplitude_kernel(lines, fields, basis, out, fbuf, bbuf, mine, parts, stack, load_sems,
@@ -121,9 +121,16 @@
         for step, device in enumerate(line_devices):
             begin(slot, slot, line_send.at[p * lines + step], line_recv.at[p * lines + line], device)
 
+    def drain():
+        while started:
+            started.pop().wait_send()
+
     def place(k, p):
         return out.at[pl.ds(pl.multiple_of(order[k] * block + starts[p], 8), sizes[p])]
 
+    line_copies = started[-len(pieces) * (lines - 1):]
+    del started[-len(pieces) * (lines - 1):]
+    drain()
     for p in pieces:
         for step, source in enumerate(line_sources):
             slot = stack.at[source, rows_of(p)]
@@ -135,12 +142,13 @@
         place(7, p)[...] = total
         for k in range(7):
             begin(place(7, p), place(7, p), back_send.at[p * 7 + k], back_recv.at[p * 7 + k], plane_peers[k])
+    for copy in line_copies:
+        copy.wait_send()
     for p in pieces:
         for k in reversed(range(7)):
             send(place(k, p), place(k, p), back_send.at[p * 7 + k], back_recv.at[p * 7 + k],
                  plane_peers[k]).wait_recv()
-    for copy in started:
-        copy.wait_send()
+    drain()
 
 
 def summed_amplitudes(lines, fields, basis):

time: 23.9 us -> 24.3 us (1.017)
  Pallas kernels: 23.1 us -> 23.5 us
    pallas_call x1, Pallas kernels: 18 us -> 18.4 us  [summed_amplitudes(): pl.pallas_call(functools.partial(amplitude_kernel, lines), out_shape=jax....]
where the time goes in v6:
time: 24.3 us; the launch traced here: 24.1 us
  Pallas kernels  23.5 us (97%)
  between operations  0.65 us (3%)
    pallas_call x1, Pallas kernels, summed_amplitudes(): pl.pallas_call(functools.partial(amplitude_kernel, lines), out_shape=jax....  18.4 us
    pallas_call x1, Pallas kernels, regimes_of(): pl.pallas_call(regime_kernel, out_shape=(jax.ShapeDtypeStruct((regimes, d...  5.1 us

profile of v6, /device:TPU:0, one launch (start us, length us, event | category | flops | bytes accessed | tf_op | source)
XLA Modules:
  0.0 24.1 jit_solution(13769750711172923523)
XLA Ops:
  0.6 0.0 copy-start
  0.6 18.4 %shard_map.58.amplitudes = f32[384,128]{1,0:T(8,128)S(1)} custom-call(bf16[384,4096]{1,0:T(8,128)(2,1)} %fields.3, bf16[4096,128]{1,0:T(8,128)(2,1)} %basis.1), custom_call_target="tpu_custom_call" | custom-call | flops 402653184 | bytes 4194304 | tf_op jit(solution)/shard_map/pallas_call | solution.py:160
  19.0 0.0 copy-done
  19.0 5.1 %shard_map.59 = (f32[16,384]{1,0:T(8,128)}, f32[16,128]{1,0:T(8,128)}, f32[16,4096]{1,0:T(8,128)}) custom-call(s32[16]{0:T(128)S(1)} %copy-done, f32[384,128]{1,0:T(8,128)S(1)} %shard_map.58.amplitudes, bf16[384,4096]{1,0:T(8,128)(2,1)} %fields.3), custom_call_target="tpu_custom_call" | custom-call | flops 50331648 | bytes 3145728 | tf_op jit(solution)/shard_map/pallas_call | solution.py:265
Async XLA Ops:
  0.6 18.4 %copy-start = (s32[16]{0:T(128)S(1)}, s32[16]{0:T(128)}, u32[]{:S(2)}) copy-start(s32[16]{0:T(128)} %seeds.1) | copy-start | bytes 196

commit v7 on v6

--- a/solution.py
+++ b/solution.py
@@ -11,6 +11,7 @@
 CHUNKS = 2
 VMEM_BYTES = 53 * 1024 * 1024
 COLUMNS = 1024
+DEPTH_CHUNKS = 8
 NT = (((1,), (1,)), ((), ()))
 
 
@@ -70,21 +71,19 @@
     for device in line_devices + plane_peers:
         pl.semaphore_signal(barrier, inc=1, device_id={"grid": device}, device_id_type=pl.DeviceIdType.MESH)
 
+    depth = basis.shape[0] // DEPTH_CHUNKS
+    loads = []
+    for i in range(DEPTH_CHUNKS):
+        part = pl.ds(i * depth, depth)
+        pair = (pltpu.make_async_copy(basis.at[part], bbuf.at[part], load_sems.at[2 * i]),
+                pltpu.make_async_copy(fields.at[:, part], fbuf.at[:, part], load_sems.at[2 * i + 1]))
+        for load in pair:
+            load.start()
+        loads.append(pair)
+
     sizes = piece_sizes(block)
     starts = [sum(sizes[:p]) for p in range(len(sizes))]
     pieces = range(len(sizes))
-    basis_load = pltpu.make_async_copy(basis, bbuf, load_sems.at[0])
-    basis_load.start()
-    loads = {}
-    for p in pieces:
-        for k in range(8):
-            first = pl.multiple_of(order[k] * block + starts[p], 16)
-            load = pltpu.make_async_copy(
-                fields.at[pl.ds(first, sizes[p])], fbuf.at[pl.ds(8 * starts[p] + k * sizes[p], sizes[p])],
-                load_sems.at[1 + p * 8 + k])
-            load.start()
-            loads[p, k] = load
-
     started = []
 
     def begin(*what):
@@ -96,23 +95,28 @@
     def rows_of(p):
         return pl.ds(starts[p], sizes[p])
 
-    basis_load.wait()
+    total = None
+    for i in range(DEPTH_CHUNKS):
+        for load in loads[i]:
+            load.wait()
+        part = slice(i * depth, (i + 1) * depth)
+        term = jnp.dot(fbuf[:, part], bbuf[part, :], preferred_element_type=jnp.float32)
+        total = term if total is None else total + term
+    mine[...] = total
+
+    def block_rows(k, p):
+        return pl.ds(pl.multiple_of(order[k] * block + starts[p], 8), sizes[p])
+
+    pl.semaphore_wait(barrier, 7 + lines - 1)
     plane_copies = {}
     for p in pieces:
-        for k in range(8):
-            loads[p, k].wait()
-        span = slice(8 * starts[p], 8 * (starts[p] + sizes[p]))
-        mine[span, :] = jnp.dot(fbuf[span, :], bbuf[...], preferred_element_type=jnp.float32)
-        if p == 0:
-            pl.semaphore_wait(barrier, 7 + lines - 1)
         for k in range(7):
             plane_copies[p, k] = begin(
-                mine.at[pl.ds(8 * starts[p] + k * sizes[p], sizes[p])], parts.at[k, rows_of(p)],
+                mine.at[block_rows(k, p)], parts.at[k, rows_of(p)],
                 plane_send.at[p * 7 + k], plane_recv.at[p * 7 + k], plane_peers[k])
 
     for p in pieces:
-        first = 8 * starts[p] + 7 * sizes[p]
-        total = mine[first:first + sizes[p], :]
+        total = mine[block_rows(7, p), :]
         for k in reversed(range(7)):
             plane_copies[p, k].wait_recv()
             total = total + parts[k, rows_of(p), :]
@@ -126,7 +130,7 @@
             started.pop().wait_send()
 
     def place(k, p):
-        return out.at[pl.ds(pl.multiple_of(order[k] * block + starts[p], 8), sizes[p])]
+        return out.at[block_rows(k, p)]
 
     line_copies = started[-len(pieces) * (lines - 1):]
     del started[-len(pieces) * (lines - 1):]
@@ -168,7 +172,7 @@
             pltpu.VMEM((rows, eofs), jnp.float32),
             pltpu.VMEM((7, block, eofs), jnp.float32),
             pltpu.VMEM((lines, block, eofs), jnp.float32),
-            dma((1 + 8 * pieces,)), dma((7 * pieces,)), dma((7 * pieces,)),
+            dma((2 * DEPTH_CHUNKS,)), dma((7 * pieces,)), dma((7 * pieces,)),
             dma((lines * pieces,)), dma((lines * pieces,)), dma((7 * pieces,)), dma((7 * pieces,)),
         ],
         compiler_params=pltpu.CompilerParams(
@@ -289,7 +293,7 @@
 def on_device(mesh, fields, eof_basis, seed_days):
     n = mesh.shape["grid"]
     day_rows = fields.shape[0]
-    if n % 8 == 0 and n > 8 and day_rows % 128 == 0:
+    if n % 8 == 0 and n > 8 and day_rows % 128 == 0 and fields.shape[1] % (256 * DEPTH_CHUNKS) == 0:
         amplitudes = summed_amplitudes(n // 8, fields, eof_basis)
     else:
         partial_value = jnp.dot(fields, eof_basis, preferred_element_type=jnp.float32)

time: 24.3 us -> 25.1 us (1.033)
  Pallas kernels: 23.5 us -> 24.3 us
    pallas_call x1, Pallas kernels: 18.4 us -> 19.2 us  [summed_amplitudes(): pl.pallas_call(functools.partial(amplitude_kernel, lines), out_shape=jax....]
where the time goes in v7:
time: 25.1 us; the launch traced here: 24.9 us
  Pallas kernels  24.3 us (97%)
  between operations  0.65 us (3%)
    pallas_call x1, Pallas kernels, summed_amplitudes(): pl.pallas_call(functools.partial(amplitude_kernel, lines), out_shape=jax....  19.2 us
    pallas_call x1, Pallas kernels, regimes_of(): pl.pallas_call(regime_kernel, out_shape=(jax.ShapeDtypeStruct((regimes, d...  5.1 us

profile of v7, /device:TPU:0, one launch (start us, length us, event | category | flops | bytes accessed | tf_op | source)
XLA Modules:
  0.0 24.9 jit_solution(15481300143069280956)
XLA Ops:
  0.6 0.0 copy-start
  0.6 19.2 %shard_map.58.amplitudes = f32[384,128]{1,0:T(8,128)S(1)} custom-call(bf16[384,4096]{1,0:T(8,128)(2,1)} %fields.3, bf16[4096,128]{1,0:T(8,128)(2,1)} %basis.1), custom_call_target="tpu_custom_call" | custom-call | flops 402653184 | bytes 4194304 | tf_op jit(solution)/shard_map/pallas_call | solution.py:164
  19.8 0.0 copy-done
  19.8 5.1 %shard_map.59 = (f32[16,384]{1,0:T(8,128)}, f32[16,128]{1,0:T(8,128)}, f32[16,4096]{1,0:T(8,128)}) custom-call(s32[16]{0:T(128)S(1)} %copy-done, f32[384,128]{1,0:T(8,128)S(1)} %shard_map.58.amplitudes, bf16[384,4096]{1,0:T(8,128)(2,1)} %fields.3), custom_call_target="tpu_custom_call" | custom-call | flops 50331648 | bytes 3145728 | tf_op jit(solution)/shard_map/pallas_call | solution.py:269
Async XLA Ops:
  0.6 19.2 %copy-start = (s32[16]{0:T(128)S(1)}, s32[16]{0:T(128)}, u32[]{:S(2)}) copy-start(s32[16]{0:T(128)} %seeds.1) | copy-start | bytes 196

commit v8 on v6

--- a/solution.py
+++ b/solution.py
@@ -35,7 +35,7 @@
 
 
 def piece_sizes(block):
-    return [block - 16, 16] if block > 16 else [block]
+    return [16] * (block // 16)
 
 
 def amplitude_kernel(lines, fields, basis, out, fbuf, bbuf, mine, parts, stack, load_sems,

time: 24.3 us -> 23.9 us (0.984)
  Pallas kernels: 23.5 us -> 23.1 us
    pallas_call x1, Pallas kernels: 18.4 us -> 18 us  [summed_amplitudes(): pl.pallas_call(functools.partial(amplitude_kernel, lines), out_shape=jax....]
where the time goes in v8:
time: 23.9 us; the launch traced here: 23.8 us
  Pallas kernels  23.1 us (97%)
  between operations  0.65 us (3%)
    pallas_call x1, Pallas kernels, summed_amplitudes(): pl.pallas_call(functools.partial(amplitude_kernel, lines), out_shape=jax....  18 us
    pallas_call x1, Pallas kernels, regimes_of(): pl.pallas_call(regime_kernel, out_shape=(jax.ShapeDtypeStruct((regimes, d...  5.1 us

profile of v8, /device:TPU:0, one launch (start us, length us, event | category | flops | bytes accessed | tf_op | source)
XLA Modules:
  0.0 23.8 jit_solution(16558169416834268597)
XLA Ops:
  0.6 0.0 copy-start
  0.6 18.0 %shard_map.58.amplitudes = f32[384,128]{1,0:T(8,128)S(1)} custom-call(bf16[384,4096]{1,0:T(8,128)(2,1)} %fields.3, bf16[4096,128]{1,0:T(8,128)(2,1)} %basis.1), custom_call_target="tpu_custom_call" | custom-call | flops 402653184 | bytes 4194304 | tf_op jit(solution)/shard_map/pallas_call | solution.py:160
  18.6 0.0 copy-done
  18.7 5.1 %shard_map.59 = (f32[16,384]{1,0:T(8,128)}, f32[16,128]{1,0:T(8,128)}, f32[16,4096]{1,0:T(8,128)}) custom-call(s32[16]{0:T(128)S(1)} %copy-done, f32[384,128]{1,0:T(8,128)S(1)} %shard_map.58.amplitudes, bf16[384,4096]{1,0:T(8,128)(2,1)} %fields.3), custom_call_target="tpu_custom_call" | custom-call | flops 50331648 | bytes 3145728 | tf_op jit(solution)/shard_map/pallas_call | solution.py:265
Async XLA Ops:
  0.6 18.0 %copy-start = (s32[16]{0:T(128)S(1)}, s32[16]{0:T(128)}, u32[]{:S(2)}) copy-start(s32[16]{0:T(128)} %seeds.1) | copy-start | bytes 196

commit v9 on v8

--- a/solution.py
+++ b/solution.py
@@ -11,6 +11,7 @@
 CHUNKS = 2
 VMEM_BYTES = 53 * 1024 * 1024
 COLUMNS = 1024
+BASIS_COPIES = 4
 NT = (((1,), (1,)), ((), ()))
 
 
@@ -73,15 +74,20 @@
     sizes = piece_sizes(block)
     starts = [sum(sizes[:p]) for p in range(len(sizes))]
     pieces = range(len(sizes))
-    basis_load = pltpu.make_async_copy(basis, bbuf, load_sems.at[0])
-    basis_load.start()
+    depth = basis.shape[0] // BASIS_COPIES
+    basis_loads = []
+    for i in range(BASIS_COPIES):
+        part = pl.ds(i * depth, depth)
+        load = pltpu.make_async_copy(basis.at[part], bbuf.at[part], load_sems.at[i])
+        load.start()
+        basis_loads.append(load)
     loads = {}
     for p in pieces:
         for k in range(8):
             first = pl.multiple_of(order[k] * block + starts[p], 16)
             load = pltpu.make_async_copy(
                 fields.at[pl.ds(first, sizes[p])], fbuf.at[pl.ds(8 * starts[p] + k * sizes[p], sizes[p])],
-                load_sems.at[1 + p * 8 + k])
+                load_sems.at[BASIS_COPIES + p * 8 + k])
             load.start()
             loads[p, k] = load
 
@@ -96,7 +102,8 @@
     def rows_of(p):
         return pl.ds(starts[p], sizes[p])
 
-    basis_load.wait()
+    for load in basis_loads:
+        load.wait()
     plane_copies = {}
     for p in pieces:
         for k in range(8):
@@ -168,7 +175,7 @@
             pltpu.VMEM((rows, eofs), jnp.float32),
             pltpu.VMEM((7, block, eofs), jnp.float32),
             pltpu.VMEM((lines, block, eofs), jnp.float32),
-            dma((1 + 8 * pieces,)), dma((7 * pieces,)), dma((7 * pieces,)),
+            dma((BASIS_COPIES + 8 * pieces,)), dma((7 * pieces,)), dma((7 * pieces,)),
             dma((lines * pieces,)), dma((lines * pieces,)), dma((7 * pieces,)), dma((7 * pieces,)),
         ],
         compiler_params=pltpu.CompilerParams(
@@ -289,7 +296,7 @@
 def on_device(mesh, fields, eof_basis, seed_days):
     n = mesh.shape["grid"]
     day_rows = fields.shape[0]
-    if n % 8 == 0 and n > 8 and day_rows % 128 == 0:
+    if n % 8 == 0 and n > 8 and day_rows % 128 == 0 and eof_basis.shape[0] % (16 * BASIS_COPIES) == 0:
         amplitudes = summed_amplitudes(n // 8, fields, eof_basis)
     else:
         partial_value = jnp.dot(fields, eof_basis, preferred_element_type=jnp.float32)

time: 23.9 us -> 23.9 us (level)
  no operation moved by 1% of the time
where the time goes in v9:
time: 23.9 us; the launch traced here: 23.8 us
  Pallas kernels  23.1 us (97%)
  between operations  0.65 us (3%)
    pallas_call x1, Pallas kernels, summed_amplitudes(): pl.pallas_call(functools.partial(amplitude_kernel, lines), out_shape=jax....  18 us
    pallas_call x1, Pallas kernels, regimes_of(): pl.pallas_call(regime_kernel, out_shape=(jax.ShapeDtypeStruct((regimes, d...  5.1 us

profile of v9, /device:TPU:0, one launch (start us, length us, event | category | flops | bytes accessed | tf_op | source)
XLA Modules:
  0.0 23.8 jit_solution(16183090489778545606)
XLA Ops:
  0.6 0.0 copy-start
  0.6 18.0 %shard_map.58.amplitudes = f32[384,128]{1,0:T(8,128)S(1)} custom-call(bf16[384,4096]{1,0:T(8,128)(2,1)} %fields.3, bf16[4096,128]{1,0:T(8,128)(2,1)} %basis.1), custom_call_target="tpu_custom_call" | custom-call | flops 402653184 | bytes 4194304 | tf_op jit(solution)/shard_map/pallas_call | solution.py:167
  18.7 0.0 copy-done
  18.7 5.1 %shard_map.59 = (f32[16,384]{1,0:T(8,128)}, f32[16,128]{1,0:T(8,128)}, f32[16,4096]{1,0:T(8,128)}) custom-call(s32[16]{0:T(128)S(1)} %copy-done, f32[384,128]{1,0:T(8,128)S(1)} %shard_map.58.amplitudes, bf16[384,4096]{1,0:T(8,128)(2,1)} %fields.3), custom_call_target="tpu_custom_call" | custom-call | flops 50331648 | bytes 3145728 | tf_op jit(solution)/shard_map/pallas_call | solution.py:272
Async XLA Ops:
  0.6 18.0 %copy-start = (s32[16]{0:T(128)S(1)}, s32[16]{0:T(128)}, u32[]{:S(2)}) copy-start(s32[16]{0:T(128)} %seeds.1) | copy-start | bytes 196
